TPU v7x, 512 devices: a whole 4x8x8 slice. The times are simulated.
512 devices in a mesh: pin: 64 (over y, z), grp: 8 (over x, core).
Axes of the slice: x: 4, y: 8, z: 8, core: 2. Of those that a mesh axis runs over, the one named last changes fastest.
Arguments:
- slab: bfloat16 [65536, 512], P('pin'), may hold values from -6 to 6
- scales: bfloat16 [65536, 4], P('pin'), may hold values from 0.25 to 4
- owner: int32 [1081344, 1], P(('pin', 'grp')), may hold values from 0 to 63; in each aligned block of 2112 rows (0 to 2111, 2112 to 4223, ...) at most 77 rows name the same one
- local: int32 [1081344, 1], P(('pin', 'grp')), may hold values from 0 to 1023
- importance: float32 [98304, 10], P(('pin', 'grp')), may hold values from 0.05 to 1
- q_weight: bfloat16 [512, 1024], replicated, may hold values from -0.25 to 0.25
- q_bias: float32 [1024], replicated, may hold values from -3 to 3
- w_weight: bfloat16 [1536, 1024], P('pin'), may hold values from -0.15625 to 0.15625
- w_bias: float32 [1024], replicated, may hold values from -3 to 3
Outputs:
- embedded: bfloat16 [98304, 1024], P(('pin', 'grp'))
- grad_q: float32 [512, 1024], replicated
- grad_bias: float32 [1024], replicated
- loss: float32 [], replicated
Inputs may be any that keep to these rules, and one draw needn't show every extreme that they name: In the 2112 rows of one device no owner is named more than 77 times, a bound that some block reaches.
All inputs are finite; a program needn't handle non-finite values.
Results may differ from a plain program's by a relative error of at most 0.011.
Values may be sent and summed in bfloat16 or wider, within the bound.
No kernel may reach another device: no remote copies, remote signals or barrier semaphores. Data moves between devices by JAX's collectives and lax.ppermute only.
A program may use at most 128 MiB of HBM per device.

v0:
```python
import jax
import jax.numpy as jnp
from jax import lax
from jax.sharding import PartitionSpec as P

K = 10
PAIRS = 64
NEG_DEV = 64


margin = 0.5
score_scale = 8.0
epsilon = 1e-05


def silu_slope(value):
    gate = jax.nn.sigmoid(value)
    return gate * (1.0 + value * (1.0 - gate))


def body(slab, scales, owner, local, importance, q_weight, q_bias, w_weight, w_bias):
    pin_count = lax.axis_size("pin")
    group_size = lax.axis_size("grp")
    request_rows = owner.shape[0]
    capacity = request_rows * 7 // (pin_count * 3)
    targets = importance.shape[0]
    feature_width = slab.shape[1]
    hidden_width = q_weight.shape[1]
    scale_block = feature_width // scales.shape[1]
    group_negatives = NEG_DEV * group_size
    destination = owner[:, 0]
    row_ids = local[:, 0]
    onehot = (destination[:, None] == jnp.arange(pin_count, dtype=jnp.int32)[None, :]).astype(
        jnp.int32
    )
    earlier = jnp.cumsum(onehot, axis=0) - onehot
    slot_of = jnp.sum(earlier * onehot, axis=1)
    wanted = jnp.zeros((pin_count, capacity), jnp.int32).at[destination, slot_of].set(row_ids)
    asked = lax.all_to_all(wanted, "pin", split_axis=0, concat_axis=0, tiled=True)
    received = (
        lax.all_to_all(
            jnp.take(slab, asked, axis=0), "pin", split_axis=0, concat_axis=0, tiled=True
        ),
        lax.all_to_all(
            jnp.take(scales, asked, axis=0), "pin", split_axis=0, concat_axis=0, tiled=True
        ),
    )
    got_rows, got_scales = received
    factor = jnp.repeat(got_scales[destination, slot_of].astype(jnp.float32), scale_block, axis=1)
    fetched = (got_rows[destination, slot_of].astype(jnp.float32) * factor).astype(jnp.bfloat16)
    grouped = fetched.reshape(targets, K + 1, feature_width)
    own_rows = grouped[:, 0]
    near_rows = grouped[:, 1:].reshape(targets * K, feature_width)
    inner = jnp.dot(near_rows, q_weight, preferred_element_type=jnp.float32) + q_bias
    shares = importance / jnp.sum(importance, axis=1, keepdims=True)
    smooth_inner = jax.nn.silu(inner).reshape(targets, K, hidden_width)
    pooled = jnp.sum(shares[:, :, None] * smooth_inner, axis=1).astype(jnp.bfloat16)
    joined = jnp.concatenate([own_rows, pooled], axis=1)
    part = joined
    outer = (
        jnp.dot(
            part,
            lax.all_gather(w_weight, "pin", axis=0, tiled=True),
            preferred_element_type=jnp.float32,
        )
        + w_bias
    )
    active = jax.nn.silu(outer)
    scaling = lax.rsqrt(jnp.mean(active * active, axis=1, keepdims=True) + epsilon)
    embedded = (active * scaling).astype(jnp.bfloat16)
    queries = embedded[:PAIRS]
    positives = embedded[PAIRS : 2 * PAIRS]
    own_negatives = embedded[2 * PAIRS :]
    close = (
        jnp.sum(queries.astype(jnp.float32) * positives.astype(jnp.float32), axis=1) / hidden_width
    )
    coef_factor = score_scale / (group_negatives * hidden_width)
    piece = lax.all_gather(own_negatives, "grp", axis=0, tiled=True)
    far = (
        lax.dot_general(
            queries, piece, (((1,), (1,)), ((), ())), preferred_element_type=jnp.float32
        )
        / hidden_width
    )
    margins = score_scale * (far - close[:, None]) + margin
    coef = (jax.nn.sigmoid(margins) * coef_factor).astype(jnp.bfloat16)
    toward = jnp.dot(coef, piece, preferred_element_type=jnp.float32)
    row_total = jnp.sum(coef.astype(jnp.float32), axis=1)
    objective = jnp.sum(jax.nn.softplus(margins))
    coef_all, toward, row_total, objective = (coef, toward, row_total, objective)
    d_queries = toward - row_total[:, None] * positives.astype(jnp.float32)
    d_positives = -row_total[:, None] * queries.astype(jnp.float32)
    part = coef_all
    d_negatives = lax.psum_scatter(
        lax.dot_general(
            part, queries, (((0,), (0,)), ((), ())), preferred_element_type=jnp.float32
        ).astype(jnp.bfloat16),
        "grp",
        scatter_dimension=0,
        tiled=True,
    ).astype(jnp.float32)
    d_embed = jnp.concatenate([d_queries, d_positives, d_negatives], axis=0)
    along = jnp.sum(d_embed * active, axis=1, keepdims=True)
    d_active = scaling * (d_embed - active * (along * scaling * scaling / hidden_width))
    d_outer = (d_active * silu_slope(outer)).astype(jnp.bfloat16)
    d_joined = lax.dot_general(
        d_outer,
        lax.all_gather(w_weight, "pin", axis=0, tiled=True),
        (((1,), (1,)), ((), ())),
        preferred_element_type=jnp.float32,
    )
    d_pooled = d_joined[:, feature_width:]
    spread = (shares[:, :, None] * d_pooled[:, None, :]).reshape(targets * K, hidden_width)
    d_inner = (spread * silu_slope(inner)).astype(jnp.bfloat16)
    grad_q = lax.dot_general(
        near_rows, d_inner, (((0,), (0,)), ((), ())), preferred_element_type=jnp.float32
    )
    grad_bias = jnp.sum(d_inner.astype(jnp.float32), axis=0)
    grad_q, grad_bias, objective = lax.psum(
        (grad_q, grad_bias, objective / group_negatives), ("pin", "grp")
    )
    loss = objective / (PAIRS * pin_count * group_size)
    return (embedded, grad_q, grad_bias, loss)


def solution(mesh):
    in_specs = (
        P("pin", None),
        P("pin", None),
        P(("pin", "grp"), None),
        P(("pin", "grp"), None),
        P(("pin", "grp"), None),
        P(),
        P(),
        P("pin", None),
        P(),
    )
    out_specs = (P(("pin", "grp"), None), P(), P(), P())
    return jax.shard_map(body, mesh=mesh, in_specs=in_specs, out_specs=out_specs, check_vma=False)
```

profile of v0, /device:TPU:1, one launch (start us, length us, event | category | flops | bytes accessed | tf_op | source)
XLA Modules:
  0.0 780.4 jit_solution(2283540195674119833)
XLA Ops:
  8.2 18.3 %reduce-window.6 = s32[64,17,128]{2,1,0:T(8,128)S(1)} reduce-window(s32[64,17,128]{2,1,0:T(8,128)S(1)} %reshape.126, s32[]{:T(128)} %constant.32.clone.1), window={size=1x1x128 pad=0_0x0_0x127_0}, to_apply=%region_0.0 | reduce-window | flops 17686528 | bytes 1114116 | tf_op jit(solution)/shard_map/reduce-window
  30.4 11.2 %scatter_custom_fusion = s32[4928]{0:T(1024)S(1)} fusion(s32[2112]{0:T(1024)S(1)} %broadcast_select_fusion.2, s32[2112]{0:T(1024)S(1)} %reduce.3, s32[]{:T(128)} %constant.32.clone.1), kind=kCustom, calls=%fused_computation.63 | custom fusion | bytes 19716
  42.4 17.1 %all-to-all-start = ((s32[64,1,77]{2,1,0:T(1,128)}), s32[64,1,77]{2,1,0:T(1,128)S(1)}, u32[]{:S(2)}, u32[]{:S(2)}) async-start(s32[64,1,77]{2,1,0:T(1,128)} %bitcast.3), calls=%async_computation | async-start | bytes 65536 | tf_op jit(solution)/shard_map/all_to_all | solution.py:39
  59.7 10.6 %all-to-all-done = s32[64,1,77]{2,1,0:T(1,128)S(1)} async-done(((s32[64,1,77]{2,1,0:T(1,128)}), s32[64,1,77]{2,1,0:T(1,128)S(1)}, u32[]{:S(2)}, u32[]{:S(2)}) %all-to-all-start) | async-done | bytes 19744 | tf_op jit(solution)/shard_map/all_to_all | solution.py:39
  70.4 15.1 %gather_fusion = bf16[4928,512]{1,0:T(8,128)(2,1)} fusion(bf16[1024,512]{1,0:T(8,128)(2,1)S(1)} %copy-done.2, s32[5120]{0:T(1024)S(1)} %pad_clamp_fusion), kind=kCustom, calls=%fused_computation | custom fusion | bytes 10112256 | tf_op jit(solution)/shard_map/jit(_take)/gather | solution.py:42
  85.6 7.6 reshape.129
  93.2 11.2 %gather_fusion.2 = bf16[4928,4]{1,0:T(8,128)(2,1)} fusion(bf16[1024,4]{1,0:T(8,128)(2,1)S(1)} %copy.31, s32[5120]{0:T(1024)S(1)} %pad_clamp_fusion), kind=kCustom, calls=%fused_computation.2 | custom fusion | bytes 98560 | tf_op jit(solution)/shard_map/jit(_take)/gather | solution.py:45
  111.7 6.1 broadcast_select_fusion
  122.8 7.5 all-to-all-start.1
  133.4 19.6 %gather_fusion.3 = bf16[2112,4]{1,0:T(8,128)(2,1)S(1)} fusion(bf16[64,77,4]{2,0,1:T(8,128)(2,1)S(1)} %copy.34, s32[2112]{0:T(1024)S(1)} %get-tuple-element.10), kind=kCustom, calls=%fused_computation.3 | custom fusion | bytes 50688 | tf_op jit(solution)/shard_map/gather | solution.py:49
  156.9 7.0 reshape.118
  163.9 112.8 %all-to-all-done.1 = bf16[64,77,512]{2,1,0:T(8,128)(2,1)} async-done(((bf16[64,77,512]{2,1,0:T(8,128)(2,1)}), bf16[64,77,512]{2,1,0:T(8,128)(2,1)}, u32[]{:S(2)}, u32[]{:S(2)}) %all-to-all-start.1) | async-done | bytes 5046304 | tf_op jit(solution)/shard_map/all_to_all | solution.py:41
  276.7 7.6 copy.30
  284.3 34.2 %gather_fusion.1 = bf16[2112,512]{1,0:T(8,128)(2,1)S(1)} fusion(bf16[64,77,512]{2,0,1:T(8,128)(2,1)} %copy.30, s32[2112]{0:T(1024)S(1)} %get-tuple-element.10), kind=kCustom, calls=%fused_computation.1 | custom fusion | bytes 4342272 | tf_op jit(solution)/shard_map/gather | solution.py:50
  335.0 8.7 %fusion = (f32[1920,1024]{1,0:T(8,128)}, f32[1920,1024]{1,0:T(8,128)}) fusion(f32[1024]{0:T(1024)S(1)} %copy-done.9, bf16[1920,512]{1,0:T(8,128)(2,1)S(1)} %reshape.119, bf16[512,1024]{1,0:T(8,128)(2,1)S(1)} %copy-done), kind=kOutput, calls=%fused_computation.9 | convolution fusion | flops 2023096320 | bytes 18747392 | tf_op jit(solution)/shard_map/dot_general | solution.py:54
  343.7 10.4 %reshape.120 = f32[192,10,1024]{2,1,0:T(8,128)} reshape(f32[1920,1024]{1,0:T(8,128)} %get-tuple-element.14) | data formatting | bytes 15728640 | tf_op jit(solution)/shard_map/reshape | solution.py:56
  354.1 7.3 multiply_reduce_fusion
  365.5 50.8 %all-gather.5.cloned.1.call-done = bf16[512,1024]{1,0:T(8,128)(2,1)} async-done(((bf16[64,1024]{1,0:T(8,128)(2,1)}), bf16[512,1024]{1,0:T(8,128)(2,1)}) %all-gather.5.cloned.1.call-update) | async-done | bytes 1048592 | tf_op jit(solution)/shard_map/all_gather | solution.py:78
  422.7 32.4 %reduce-scatter.2.cloned.1.call-done = bf16[64,1024]{1,0:T(8,128)(2,1)} async-done(((bf16[512,1024]{1,0:T(8,128)(2,1)}), bf16[64,1024]{1,0:T(8,128)(2,1)}) %reduce-scatter.2.cloned.1.call-update) | async-done | bytes 131088 | tf_op jit(solution)/shard_map/reduce_scatter | solution.py:94
  460.0 6.2 mul.163
  466.2 11.1 %mul.164 = f32[1920,1024]{1,0:T(8,128)} reshape(f32[192,10,1024]{2,1,0:T(8,128)} %mul.163) | data formatting | bytes 15728640 | tf_op jit(solution)/shard_map/mul | solution.py:113
  477.3 7.6 convert_reduce_fusion
  489.3 101.1 %all-reduce.1 = (f32[1024]{0:T(1024)}, f32[]{:T(128)}) all-reduce(f32[1024]{0:T(1024)S(1)} %get-tuple-element.6, f32[]{:T(128)S(6)} %div.56), channel_id=1, replica_groups=mesh['pin'=64,'grp'=8] {'pin','grp'}, use_global_device_ids=true, to_apply=%region_13.14 | all-reduce | flops 1025 | bytes 8200 | tf_op jit(solution)/shard_map/psum | solution.py:119
  591.0 178.4 %all-reduce.4.cloned.1.call-done = f32[512,1024]{1,0:T(8,128)} async-done(((f32[512,1024]{1,0:T(8,128)}), f32[512,1024]{1,0:T(8,128)}) %all-reduce.4.cloned.1.call-update) | async-done | bytes 2097168 | tf_op jit(solution)/shard_map/psum | solution.py:119
  (91 shorter events, 63.9 us)
Async XLA Ops:
  7.2 327.8 %copy-start = (bf16[512,1024]{1,0:T(8,128)(2,1)S(1)}, bf16[512,1024]{1,0:T(8,128)(2,1)}, u32[]{:S(2)}) copy-start(bf16[512,1024]{1,0:T(8,128)(2,1)} %param.14) | copy-start | bytes 3145732
  26.6 3.5 copy-start.6
  26.6 3.6 copy-start.10
  26.6 3.7 copy-start.11
  26.6 3.8 copy-start.7
  26.6 32.9 %copy-start.8 = (bf16[1024,4]{0,1:T(4,128)(2,1)S(1)}, bf16[1024,4]{0,1:T(4,128)(2,1)}, u32[]{:S(2)}) copy-start(bf16[1024,4]{0,1:T(4,128)(2,1)} %param.10) | copy-start | bytes 24580
  26.6 43.8 %copy-start.2 = (bf16[1024,512]{1,0:T(8,128)(2,1)S(1)}, bf16[1024,512]{1,0:T(8,128)(2,1)}, u32[]{:S(2)}) copy-start(bf16[1024,512]{1,0:T(8,128)(2,1)} %param.9) | copy-start | bytes 3145732
  42.4 27.9 %all-to-all-start = ((s32[64,1,77]{2,1,0:T(1,128)}), s32[64,1,77]{2,1,0:T(1,128)S(1)}, u32[]{:S(2)}, u32[]{:S(2)}) async-start(s32[64,1,77]{2,1,0:T(1,128)} %bitcast.3), calls=%async_computation | async-start | bytes 65536 | tf_op jit(solution)/shard_map/all_to_all | solution.py:39
  107.1 15.7 %all-to-all-start.2 = ((bf16[64,77,4]{1,2,0:T(4,128)(2,1)}), bf16[64,77,4]{1,2,0:T(4,128)(2,1)S(1)}, u32[]{:S(2)}, u32[]{:S(2)}) async-start(bf16[64,77,4]{1,2,0:T(4,128)(2,1)} %copy.33), calls=%async_computation.2 | async-start | bytes 131072 | tf_op jit(solution)/shard_map/all_to_all | solution.py:44
  117.7 13.3 %copy-start.5 = (f32[192,10]{0,1:T(8,128)S(1)}, f32[192,10]{0,1:T(8,128)}, u32[]{:S(2)}) copy-start(f32[192,10]{0,1:T(8,128)} %param.13) | copy-start | bytes 23044
  122.8 153.9 %all-to-all-start.1 = ((bf16[64,77,512]{2,1,0:T(8,128)(2,1)}), bf16[64,77,512]{2,1,0:T(8,128)(2,1)}, u32[]{:S(2)}, u32[]{:S(2)}) async-start(bf16[64,77,512]{2,1,0:T(8,128)(2,1)} %broadcast_select_fusion), calls=%async_computation.1 | async-start | bytes 10485760 | tf_op jit(solution)/shard_map/all_to_all | solution.py:41
  130.3 231.2 %all-gather.3.cloned.1.call-start = ((), (), s32[]{:S(2)}) async-start(), calls=%async_computation.4 | async-start | bytes 3194880 | tf_op jit(solution)/shard_map/all_gather | solution.py:63
  131.0 285.3 %all-gather.5.cloned.1.call-start = ((), (), s32[]{:S(2)}) async-start(), calls=%async_computation.5 | async-start | bytes 1179648 | tf_op jit(solution)/shard_map/all_gather | solution.py:78
  330.8 4.2 copy-start.9
  354.1 7.4 copy-start.12
  364.6 58.1 %copy-start.3 = (bf16[192,1024]{1,0:T(8,128)(2,1)}, bf16[192,1024]{1,0:T(8,128)(2,1)S(1)}, u32[]{:S(2)}) copy-start(bf16[192,1024]{1,0:T(8,128)(2,1)S(1)} %multiply_convert_fusion.3) | copy-start | bytes 1179652
  365.3 89.7 %reduce-scatter.2.cloned.1.call-start = ((), (), s32[]{:S(2)}) async-start(), calls=%async_computation.6 | async-start | bytes 1179648 | tf_op jit(solution)/shard_map/reduce_scatter | solution.py:94
  418.7 1.6 copy-start.4
  420.1 349.3 %all-reduce.4.cloned.1.call-start = ((), (), s32[]{:S(2)}) async-start(), calls=%async_computation.7 | async-start | bytes 4194304 | tf_op jit(solution)/shard_map/psum | solution.py:119
  488.6 284.0 %copy-start.1 = (bf16[512,1024]{1,0:T(8,128)(2,1)S(1)}, bf16[512,1024]{1,0:T(8,128)(2,1)}, u32[]{:S(2)}) copy-start(bf16[512,1024]{1,0:T(8,128)(2,1)} %param.14) | copy-start | bytes 3145732
Sparse Core Ops, SparseCore 0:
  134.2 196.0 all-gather.2
  365.5 50.7 all-gather.4
  420.2 34.7 reduce-scatter.1
  488.7 280.6 all-reduce.3
where the time goes:
time: 790 us; the launch traced here: 780 us
  waiting for transfers between devices  391 us (49%)
  local copies, waits for them, and re-layouts  169 us (21%)
  blocking collectives  101 us (13%)
  other arithmetic  49.8 us (6%)
  starting transfers between devices  29.4 us (4%)
  matrix products  24 us (3%)
  between operations  16.9 us (2%)
    psum x1, waiting for transfers between devices, body(): lax.psum((grad_q, grad_bias, objective / group_negatives), ('pin', 'grp'))  178 us
    all_to_all x1, waiting for transfers between devices, body(): lax.all_to_all(jnp.take(slab, asked, axis=0), 'pin', split_axis=0, concat...  113 us
    psum x1, blocking collectives, body(): lax.psum((grad_q, grad_bias, objective / group_negatives), ('pin', 'grp'))  101 us
    all_gather x1, waiting for transfers between devices, body(): piece = lax.all_gather(own_negatives, 'grp', axis=0, tiled=True)  50.8 us
    gather x1, local copies, waits for them, and re-layouts, body(): got_rows[destination, slot_of].astype(jnp.float32) * factor  34.2 us
    reduce_scatter x1, waiting for transfers between devices, body(): lax.psum_scatter(lax.dot_general(part, queries, (((0,), (0,)), ((), ())),...  32.4 us
    gather x2, local copies, waits for them, and re-layouts, body(): jnp.take(slab, asked, axis=0)  22.8 us
    gather x1, local copies, waits for them, and re-layouts, body(): got_scales[destination, slot_of].astype(jnp.float32)  19.6 us
  transfers between devices with their start and end apart: 7, of which 6 were waited for; matrix products, arithmetic and copies ran while one was open for 16% of the time, Pallas kernels for 0%

commit v1 on v0

v1 whole, which is shorter than its diff:
```python
import jax
import jax.numpy as jnp
from jax import lax
from jax.experimental import pallas as pl
from jax.experimental.pallas import tpu as pltpu
from jax.sharding import Mesh
from jax.sharding import PartitionSpec as P

K = 10
PAIRS = 64
NEG_DEV = 64
SLOTS = 80
EXTRA = 128

margin = 0.5
score_scale = 8.0
epsilon = 1e-05

PIN = ("y", "z")
GRP = ("x", "core")
bf16 = jnp.bfloat16
f32 = jnp.float32
VMEM = 48 * 1024 * 1024


def sigmoid(value):
    return 0.5 * jnp.tanh(0.5 * value) + 0.5


def params():
    return pltpu.CompilerParams(vmem_limit_bytes=VMEM)


def row_dot(a, b):
    return lax.dot_general(a, b, (((1,), (1,)), ((), ())), preferred_element_type=f32)


def col_dot(a, b):
    return lax.dot_general(a, b, (((0,), (0,)), ((), ())), preferred_element_type=f32)


def plan_kernel(owner_ref, local_ref, wanted_ref, place_ref):
    blocks, width = owner_ref.shape
    owners = wanted_ref.shape[0]
    owner_ids = lax.broadcasted_iota(jnp.int32, (owners, width), 0)
    slot_ids = lax.broadcasted_iota(jnp.int32, (width, width), 0)
    earlier = (slot_ids < lax.broadcasted_iota(jnp.int32, (width, width), 1)).astype(f32).astype(bf16)
    count = jnp.zeros((owners, 1), f32)
    high_sum = jnp.zeros((owners, width), f32)
    low_sum = jnp.zeros((owners, width), f32)
    for block in range(blocks):
        own = owner_ref[block : block + 1, :]
        wide = (own == owner_ids).astype(f32)
        low_wide = wide.astype(bf16)
        before = jnp.dot(low_wide, earlier, preferred_element_type=f32) + count
        slot = jnp.sum(wide * before, axis=0, keepdims=True).astype(jnp.int32)
        count = count + jnp.sum(wide, axis=1, keepdims=True)
        there = (slot == slot_ids).astype(f32)
        local = local_ref[block : block + 1, :]
        high_sum = high_sum + row_dot(low_wide, (there * (local >> 5).astype(f32)).astype(bf16))
        low_sum = low_sum + row_dot(low_wide, (there * (local & 31).astype(f32)).astype(bf16))
        place_ref[block : block + 1, :] = own * SLOTS + slot
    wanted_ref[...] = (high_sum * 32.0 + low_sum).astype(jnp.int32)


def plan(owner, local, owners):
    rows = owner.shape[0]
    blocks = -(-rows // 128)
    spare = blocks * 128 - rows
    owner = jnp.pad(owner[:, 0], (0, spare), constant_values=owners).reshape(blocks, 128)
    local = jnp.pad(local[:, 0], (0, spare)).reshape(blocks, 128)
    wanted, place = pl.pallas_call(
        plan_kernel,
        out_shape=(
            jax.ShapeDtypeStruct((owners, 128), jnp.int32),
            jax.ShapeDtypeStruct((blocks, 128), jnp.int32),
        ),
        compiler_params=params(),
        name="plan",
    )(owner, local)
    return wanted[:, :SLOTS], place.reshape(-1)[:rows]


def dequantize_kernel(slab_ref, scales_ref, out_ref):
    block = slab_ref.shape[1] // scales_ref.shape[1]
    for part in range(scales_ref.shape[1]):
        lanes = slice(part * block, (part + 1) * block)
        scale = scales_ref[:, part : part + 1].astype(f32)
        out_ref[:, lanes] = (slab_ref[:, lanes].astype(f32) * scale).astype(bf16)


def shares_of(importance):
    return importance / jnp.sum(importance, axis=1, keepdims=True)


def column(values, at):
    lanes = lax.broadcasted_iota(jnp.int32, values.shape, 1)
    return jnp.sum(jnp.where(lanes == at, values, 0.0), axis=1, keepdims=True)


def forward_kernel(
    own_ref,
    near_ref,
    importance_ref,
    q_weight_ref,
    q_bias_ref,
    w_ref,
    w_bias_ref,
    slope_ref,
    embedded_ref,
    active_ref,
    outer_slope_ref,
    payload_ref,
    pooled,
):
    step = pl.program_id(0)
    share = column(shares_of(importance_ref[...]), step)
    inner = jnp.dot(near_ref[...], q_weight_ref[...], preferred_element_type=f32) + q_bias_ref[...]
    gate = sigmoid(inner)
    smooth = inner * gate
    slope_ref[...] = (gate + smooth * (1.0 - gate)).astype(bf16)
    term = share * smooth

    @pl.when(step == 0)
    def _():
        pooled[...] = term

    @pl.when(step > 0)
    def _():
        pooled[...] += term

    @pl.when(step == pl.num_programs(0) - 1)
    def _():
        width = own_ref.shape[1]
        hidden = active_ref.shape[1]
        outer = (
            jnp.dot(own_ref[...], w_ref[:width, :], preferred_element_type=f32)
            + jnp.dot(pooled[...].astype(bf16), w_ref[width:, :], preferred_element_type=f32)
            + w_bias_ref[...]
        )
        gate = sigmoid(outer)
        active = outer * gate
        active_ref[...] = active
        outer_slope_ref[...] = gate + active * (1.0 - gate)
        scaling = lax.rsqrt(jnp.mean(active * active, axis=1, keepdims=True) + epsilon)
        embedded = (active * scaling).astype(bf16)
        embedded_ref[...] = embedded
        queries = embedded[:PAIRS].astype(f32)
        close = jnp.sum(queries * embedded[PAIRS : 2 * PAIRS].astype(f32), axis=1, keepdims=True)
        close = close / hidden
        first = close.astype(bf16).astype(f32)
        second = (close - first).astype(bf16).astype(f32)
        third = close - first - second
        lanes = lax.broadcasted_iota(jnp.int32, (PAIRS, EXTRA), 1)
        pieces = jnp.where(
            lanes == 0, first, jnp.where(lanes == 1, second, jnp.where(lanes == 2, third, 0.0))
        )
        payload_ref[:PAIRS, :hidden] = embedded[:PAIRS]
        payload_ref[PAIRS:, :hidden] = embedded[2 * PAIRS :]
        payload_ref[:PAIRS, hidden:] = pieces.astype(bf16)
        payload_ref[PAIRS:, hidden:] = jnp.zeros((NEG_DEV, EXTRA), bf16)


def whole(shape):
    return pl.BlockSpec(shape, lambda step: (0,) * len(shape))


def forward(fetched, importance, q_weight, q_bias, w_full, w_bias):
    targets = importance.shape[0]
    width, hidden = q_weight.shape
    sent = PAIRS + NEG_DEV
    return pl.pallas_call(
        forward_kernel,
        grid=(K,),
        in_specs=[
            pl.BlockSpec((targets, width), lambda step: (0, 0)),
            pl.BlockSpec((targets, width), lambda step: (step + 1, 0)),
            whole(importance.shape),
            whole(q_weight.shape),
            whole((1, hidden)),
            whole(w_full.shape),
            whole((1, hidden)),
        ],
        out_specs=[
            pl.BlockSpec((targets, hidden), lambda step: (step, 0)),
            whole((targets, hidden)),
            whole((targets, hidden)),
            whole((targets, hidden)),
            whole((sent, hidden + EXTRA)),
        ],
        out_shape=(
            jax.ShapeDtypeStruct((targets * K, hidden), bf16),
            jax.ShapeDtypeStruct((targets, hidden), bf16),
            jax.ShapeDtypeStruct((targets, hidden), f32),
            jax.ShapeDtypeStruct((targets, hidden), f32),
            jax.ShapeDtypeStruct((sent, hidden + EXTRA), bf16),
        ),
        scratch_shapes=[pltpu.VMEM((targets, hidden), f32)],
        compiler_params=params(),
        name="forward",
    )(fetched, fetched, importance, q_weight, q_bias[None, :], w_full, w_bias[None, :])


def backward_kernel(
    fetched_ref,
    importance_ref,
    w_ref,
    slope_ref,
    embedded_ref,
    active_ref,
    outer_slope_ref,
    group_ref,
    grad_ref,
    d_pooled,
    d_inner,
    bias_sum,
    objective_sum,
):
    step = pl.program_id(0)
    targets, hidden = active_ref.shape
    members = group_ref.shape[0]
    negatives_count = members * NEG_DEV

    @pl.when(step == 0)
    def _():
        embedded = embedded_ref[...]
        queries = embedded[:PAIRS]
        positives = embedded[PAIRS : 2 * PAIRS].astype(f32)
        negatives = embedded[2 * PAIRS :]
        group_queries = group_ref[:, :PAIRS, :hidden].reshape(members * PAIRS, hidden)
        group_negatives = group_ref[:, PAIRS:, :hidden].reshape(negatives_count, hidden)
        pieces = group_ref[:, :PAIRS, hidden:].reshape(members * PAIRS, EXTRA).astype(f32)
        group_close = jnp.sum(pieces, axis=1, keepdims=True)
        coef_factor = score_scale / (negatives_count * hidden)
        wide_queries = queries.astype(f32)
        close = jnp.sum(wide_queries * positives, axis=1, keepdims=True) / hidden
        far = row_dot(queries, group_negatives) / hidden
        margins = score_scale * (far - close) + margin
        coef = (sigmoid(margins) * coef_factor).astype(bf16)
        toward = jnp.dot(coef, group_negatives, preferred_element_type=f32)
        row_total = jnp.sum(coef.astype(f32), axis=1, keepdims=True)
        softplus = jnp.maximum(margins, 0.0) + jnp.log1p(jnp.exp(-jnp.abs(margins)))
        objective = jnp.sum(jnp.sum(softplus, axis=1, keepdims=True), axis=0, keepdims=True)
        objective_sum[...] = jnp.broadcast_to(objective / negatives_count, objective_sum.shape)
        group_far = row_dot(group_queries, negatives) / hidden
        group_margins = score_scale * (group_far - group_close) + margin
        group_coef = (sigmoid(group_margins) * coef_factor).astype(bf16)
        d_embed = jnp.concatenate(
            [
                toward - row_total * positives,
                -row_total * wide_queries,
                col_dot(group_coef, group_queries),
            ],
            axis=0,
        )
        active = active_ref[...]
        scaling = lax.rsqrt(jnp.mean(active * active, axis=1, keepdims=True) + epsilon)
        along = jnp.sum(d_embed * active, axis=1, keepdims=True)
        d_active = scaling * (d_embed - active * (along * scaling * scaling / hidden))
        d_outer = (d_active * outer_slope_ref[...]).astype(bf16)
        d_pooled[...] = row_dot(d_outer, w_ref[...])
        bias_sum[...] = jnp.zeros_like(bias_sum)

    share = column(shares_of(importance_ref[...]), step)
    d_near = (share * d_pooled[...] * slope_ref[...].astype(f32)).astype(bf16)
    d_inner[pl.ds(pl.multiple_of(step * targets, targets), targets), :] = d_near
    bias_sum[...] += jnp.sum(d_near.astype(f32), axis=0, keepdims=True)

    @pl.when(step == pl.num_programs(0) - 1)
    def _():
        near = fetched_ref[targets:, :]
        for part in range(4):
            lanes = slice(part * hidden // 4, (part + 1) * hidden // 4)
            grad_ref[:, lanes] = col_dot(near, d_inner[:, lanes]).astype(bf16)
        grad_ref[:, hidden:] = jnp.zeros((grad_ref.shape[0], EXTRA), bf16)
        rows = lax.broadcasted_iota(jnp.int32, (16, EXTRA), 0)
        small = jnp.zeros((16, EXTRA), f32)
        for part in range(hidden // EXTRA):
            piece = bias_sum[:, part * EXTRA : (part + 1) * EXTRA]
            small = jnp.where(rows == part, piece, small)
        objective = objective_sum[...]
        first = objective.astype(bf16).astype(f32)
        small = jnp.where(rows == hidden // EXTRA, first, small)
        small = jnp.where(rows == hidden // EXTRA + 1, objective - first, small)
        grad_ref[:16, hidden:] = small.astype(bf16)


def backward(fetched, importance, w_full, slope, embedded, active, outer_slope, group):
    targets, hidden = active.shape
    width = fetched.shape[1]
    return pl.pallas_call(
        backward_kernel,
        grid=(K,),
        in_specs=[
            whole(fetched.shape),
            whole(importance.shape),
            whole((hidden, hidden)),
            pl.BlockSpec((targets, hidden), lambda step: (step, 0)),
            whole(embedded.shape),
            whole(active.shape),
            whole(outer_slope.shape),
            whole(group.shape),
        ],
        out_specs=whole((width, hidden + EXTRA)),
        out_shape=jax.ShapeDtypeStruct((width, hidden + EXTRA), bf16),
        scratch_shapes=[
            pltpu.VMEM((targets, hidden), f32),
            pltpu.VMEM((targets * K, hidden), bf16),
            pltpu.VMEM((1, hidden), f32),
            pltpu.VMEM((1, EXTRA), f32),
        ],
        compiler_params=params(),
        name="backward",
    )(fetched, importance, w_full[width:], slope, embedded, active, outer_slope, group)


def exchange(values, axes):
    return lax.all_to_all(values, axes, split_axis=0, concat_axis=0, tiled=True)


def spread(values, axes):
    count = lax.axis_size(axes)
    return exchange(jnp.broadcast_to(values[None], (count,) + values.shape), axes)


def both_cores(values):
    other = lax.ppermute(values, "core", [(0, 1), (1, 0)])
    first = lax.axis_index("core") == 0
    return jnp.stack([jnp.where(first, values, other), jnp.where(first, other, values)])


def total(values, axes):
    count = lax.axis_size(axes)
    share = values.shape[0] // count
    parts = exchange(values.reshape((count, share) + values.shape[1:]), axes)
    return jnp.sum(parts.astype(f32), axis=0)


def body(slab, scales, owner, local, importance, q_weight, q_bias, w_weight, w_bias):
    pin_count = lax.axis_size(PIN)
    targets = importance.shape[0]
    width, hidden = q_weight.shape
    w_full = lax.all_gather(w_weight, PIN, axis=0, tiled=True)
    wanted, place = plan(owner, local, pin_count)
    ready = pl.pallas_call(
        dequantize_kernel,
        out_shape=jax.ShapeDtypeStruct(slab.shape, bf16),
        compiler_params=params(),
        name="dequantize",
    )(slab, scales)
    asked = exchange(wanted, PIN)
    picked = jnp.take(ready, asked.reshape(-1), axis=0, mode="clip")
    got = exchange(picked.reshape(pin_count, SLOTS, width), PIN).reshape(-1, width)
    by_neighbour = place.reshape(targets, K + 1).T.reshape(-1)
    fetched = jnp.take(got, by_neighbour, axis=0, mode="clip")
    slope, embedded, active, outer_slope, payload = forward(
        fetched, importance, q_weight, q_bias, w_full, w_bias
    )
    group = both_cores(spread(payload, "x"))
    group = group.reshape((-1,) + payload.shape)
    grads = backward(fetched, importance, w_full, slope, embedded, active, outer_slope, group)
    grads = total(grads, "core").astype(bf16)
    grads = total(grads, "x").astype(bf16)
    grads = total(grads, PIN)
    loss_row = hidden // EXTRA
    split = grads.astype(bf16)
    grads = spread(split, PIN).reshape(-1, hidden + EXTRA)
    grads = spread(grads, "x").reshape(-1, hidden + EXTRA)
    grads = both_cores(grads).reshape(-1, hidden + EXTRA)
    grad_q = grads[:, :hidden].astype(f32)
    grad_bias = grads[:loss_row, hidden:].astype(f32).reshape(-1)
    objective = jnp.sum(grads[loss_row : loss_row + 2, hidden].astype(f32))
    devices = pin_count * lax.axis_size(GRP)
    loss = objective / (PAIRS * devices)
    return (embedded, grad_q, grad_bias, loss)


def solution(mesh):
    devices = mesh.devices.reshape(8, 8, 4, 2)
    fine = Mesh(devices, PIN + GRP)
    in_specs = (
        P(PIN, None),
        P(PIN, None),
        P(PIN + GRP, None),
        P(PIN + GRP, None),
        P(PIN + GRP, None),
        P(),
        P(),
        P(PIN, None),
        P(),
    )
    out_specs = (P(PIN + GRP, None), P(), P(), P())
    return jax.shard_map(body, mesh=fine, in_specs=in_specs, out_specs=out_specs, check_vma=False)
```

time: 790 us -> 415 us (0.53); the launches traced: 780 us -> 414 us
  waiting for transfers between devices: 391 us -> 205 us
  local copies, waits for them, and re-layouts: 169 us -> 37.4 us
  other arithmetic: 49.8 us -> 11.5 us
  Pallas kernels: 0 us -> 28.2 us
  matrix products: 24 us -> 0 us
  blocking collectives: 101 us -> 78.1 us
  starting transfers between devices: 29.4 us -> 37.4 us
    psum x1 -> x0, waiting for transfers between devices: 178 us -> none  [body(): lax.psum((grad_q, grad_bias, objective / group_negatives), ('pin', 'grp'))]
    psum x1 -> x0, blocking collectives: 101 us -> none  [body(): lax.psum((grad_q, grad_bias, objective / group_negatives), ('pin', 'grp'))]
    all_to_all x0 -> x6, blocking collectives: none -> 78.1 us  [exchange(): return lax.all_to_all(values, axes, split_axis=0, concat_axis=0, tiled=True)]
    gather x7 -> x2, local copies, waits for them, and re-layouts: 89.7 us -> 31.8 us  [the longest x1 21.4 us: body(): picked = jnp.take(ready, asked.reshape(-1), axis=0, mode='clip')]
    reduce_scatter x1 -> x0, waiting for transfers between devices: 32.4 us -> none  [body(): lax.psum_scatter(lax.dot_general(part, queries, (((0,), (0,)), ((), ())),...]
    pallas_call x0 -> x4, Pallas kernels: none -> 28.2 us  [the longest x1 13.3 us: backward(): pl.pallas_call(backward_kernel, grid=(K,), in_specs=[whole(fetched.shape)...]
    all_to_all x3 -> x2, waiting for transfers between devices: 128 us -> 154 us  [exchange(): return lax.all_to_all(values, axes, split_axis=0, concat_axis=0, tiled=True)]
    dot_general x7 -> x0, matrix products: 24 us -> none  [the longest x1 8.66 us: body(): jnp.dot(near_rows, q_weight, preferred_element_type=jnp.float32) + q_bias]
  transfers between devices with their start and end apart: 7 -> 5, of which waited for: 6 -> 5; matrix products, arithmetic and copies ran while one was open for 16% -> 3% of each run, Pallas kernels for 0% -> 0%
where the time goes in v1:
time: 415 us; the launch traced here: 414 us
  waiting for transfers between devices  205 us (49%)
  blocking collectives  78.1 us (19%)
  local copies, waits for them, and re-layouts  37.4 us (9%)
  starting transfers between devices  37.4 us (9%)
  Pallas kernels  28.2 us (7%)
  between operations  16.1 us (4%)
  other arithmetic  11.5 us (3%)
    all_to_all x2, waiting for transfers between devices, exchange(): return lax.all_to_all(values, axes, split_axis=0, concat_axis=0, tiled=True)  154 us
    all_to_all x6, blocking collectives, exchange(): return lax.all_to_all(values, axes, split_axis=0, concat_axis=0, tiled=True)  78.1 us
    all_gather x1, waiting for transfers between devices, body(): w_full = lax.all_gather(w_weight, PIN, axis=0, tiled=True)  46.1 us
    all_to_all x2, starting transfers between devices, exchange(): return lax.all_to_all(values, axes, split_axis=0, concat_axis=0, tiled=True)  22.9 us
    gather x1, local copies, waits for them, and re-layouts, body(): picked = jnp.take(ready, asked.reshape(-1), axis=0, mode='clip')  21.4 us
    ppermute x2, starting transfers between devices, both_cores(): other = lax.ppermute(values, 'core', [(0, 1), (1, 0)])  14.4 us
    pallas_call x1, Pallas kernels, backward(): pl.pallas_call(backward_kernel, grid=(K,), in_specs=[whole(fetched.shape)...  13.3 us
    pallas_call x1, Pallas kernels, forward(): pl.pallas_call(forward_kernel, grid=(K,), in_specs=[pl.BlockSpec((targets...  10.5 us
  transfers between devices with their start and end apart: 5, of which 5 were waited for; matrix products, arithmetic and copies ran while one was open for 3% of the time, Pallas kernels for 0%

profile of v1, /device:TPU:1, one launch (start us, length us, event | category | flops | bytes accessed | tf_op | source)
XLA Modules:
  0.0 414.0 jit_solution(6811993481285127058)
XLA Ops:
  8.6 4.0 plan.1
  12.6 17.1 %all-to-all-start = ((s32[64,1,80]{2,1,0:T(1,128)}), s32[64,1,80]{2,1,0:T(1,128)S(1)}, u32[]{:S(2)}, u32[]{:S(2)}) async-start(s32[64,1,80]{2,1,0:T(1,128)} %bitcast.3), calls=%async_computation | async-start | bytes 65536 | tf_op jit(solution)/shard_map/all_to_all | solution.py:318
  32.3 8.2 %all-to-all-done = s32[64,1,80]{2,1,0:T(1,128)S(1)} async-done(((s32[64,1,80]{2,1,0:T(1,128)}), s32[64,1,80]{2,1,0:T(1,128)S(1)}, u32[]{:S(2)}, u32[]{:S(2)}) %all-to-all-start) | async-done | bytes 20512 | tf_op jit(solution)/shard_map/all_to_all | solution.py:318
  41.9 21.4 %gather_fusion = bf16[5120,512]{1,0:T(8,128)(2,1)} fusion(bf16[1024,512]{1,0:T(8,128)(2,1)S(1)} %dequantize.1, s32[5120]{0:T(1024)S(1)} %broadcast_clamp_fusion), kind=kCustom, calls=%fused_computation | custom fusion | bytes 10506240 | tf_op jit(solution)/shard_map/jit(_take)/gather | solution.py:352
  63.2 5.8 %all-to-all-start.1 = ((bf16[64,80,512]{2,1,0:T(8,128)(2,1)}), bf16[64,80,512]{2,1,0:T(8,128)(2,1)}, u32[]{:S(2)}, u32[]{:S(2)}) async-start(bf16[64,80,512]{2,1,0:T(8,128)(2,1)} %bitcast.43), calls=%async_computation.1 | async-start | bytes 10485760 | tf_op jit(solution)/shard_map/all_to_all | solution.py:318
  70.3 146.1 %all-to-all-done.1 = bf16[64,80,512]{2,1,0:T(8,128)(2,1)} async-done(((bf16[64,80,512]{2,1,0:T(8,128)(2,1)}), bf16[64,80,512]{2,1,0:T(8,128)(2,1)}, u32[]{:S(2)}, u32[]{:S(2)}) %all-to-all-start.1) | async-done | bytes 5242912 | tf_op jit(solution)/shard_map/all_to_all | solution.py:318
  216.3 10.4 %gather_fusion.1 = bf16[2112,512]{1,0:T(8,128)(2,1)S(1)} fusion(bf16[5120,512]{1,0:T(8,128)(2,1)} %bitcast.5, s32[3072]{0:T(1024)S(1)} %pad_clamp_fusion), kind=kCustom, calls=%fused_computation.1 | custom fusion | bytes 4333824 | tf_op jit(solution)/shard_map/jit(_take)/gather | solution.py:355
  226.8 46.1 %all-gather.2.cloned.1.call-done.w_ref = bf16[1536,1024]{1,0:T(8,128)(2,1)} async-done(((bf16[24,1024]{1,0:T(8,128)(2,1)}), bf16[1536,1024]{1,0:T(8,128)(2,1)}) %all-gather.2.cloned.1.call-update) | async-done | bytes 3145744 | tf_op jit(solution)/shard_map/all_gather | solution.py:343
  272.9 10.5 %forward.1 = (bf16[1920,1024]{1,0:T(8,128)(2,1)}, bf16[192,1024]{1,0:T(8,128)(2,1)}, f32[192,1024]{1,0:T(8,128)S(1)}, f32[192,1024]{1,0:T(8,128)S(1)}, bf16[128,1152]{1,0:T(8,128)(2,1)S(1)}) custom-call(bf16[2112,512]{1,0:T(8,128)(2,1)S(1)} %gather_fusion.1, bf16[2112,512]{1,0:T(8,128)(2,1)S(1)} %gather_fusion.1, f32[192,10]{1,0:T(8,128)S(1)} %copy.34.importance_ref, ...), custom_call_target="tpu_custom_call" | custom-call | tf_op jit(solution)/shard_map/forward/pallas_call | solution.py:172
  283.5 16.1 %all_to_all.44 = bf16[4,128,1152]{2,1,0:T(8,128)(2,1)} all-to-all(bf16[4,128,1152]{2,1,0:T(8,128)(2,1)S(1)} %broadcast_in_dim.37), channel_id=1, replica_groups=mesh['y'=8,'z'=8,'x'=4,'core'=2] {'x'}, dimensions={0} | all-to-all | bytes 2359296 | tf_op jit(solution)/shard_map/all_to_all | solution.py:318
  299.6 7.4 %collective-permute-start = (bf16[4,128,1152]{2,1,0:T(8,128)(2,1)}, bf16[4,128,1152]{2,1,0:T(8,128)(2,1)}, u32[]{:S(2)}, u32[]{:S(2)}) collective-permute-start(bf16[4,128,1152]{2,1,0:T(8,128)(2,1)} %all_to_all.44), channel_id=1, source_target_pairs={{0,1},{1,0},{2,3},{3,2},{4,5},{5,4},{6,7},{7,6},{8,9},{9,8},{10,11... | collective-permute-start | bytes 3538952 | tf_op jit(solution)/shard_map/ppermute | solution.py:327
  307.2 2.6 collective-permute-done
  309.8 1.8 select_bitcast_fusion.1
  311.7 1.7 pad_maximum_fusion
  313.9 13.3 %backward.1 = bf16[512,1152]{1,0:T(8,128)(2,1)S(1)} custom-call(bf16[2112,512]{1,0:T(8,128)(2,1)} %copy-done, f32[192,10]{1,0:T(8,128)S(1)} %copy.34.importance_ref, bf16[1024,1024]{1,0:T(8,128)(2,1)S(1)} %slice.29.w_ref, bf16[1920,1024]{1,0:T(8,128)(2,1)} %get-tuple-element.14.slope_ref, bf16[192,1024]{1,0:T(8,128)(2,1)S(1)} %copy-done.7, ...), custom_call_target="tpu_custom_call" | custom-call | tf_op jit(solution)/shard_map/backward/pallas_call | solution.py:291
  327.2 4.9 %all_to_all.45 = bf16[2,256,1152]{2,1,0:T(8,128)(2,1)S(1)} all-to-all(bf16[2,256,1152]{2,1,0:T(8,128)(2,1)S(1)} %bitcast.39), channel_id=1, replica_groups=mesh['y'=8,'z'=8,'x'=4,'core'=2] {'core'}, dimensions={0} | all-to-all | bytes 2359296 | tf_op jit(solution)/shard_map/all_to_all | solution.py:318
  332.4 12.0 %all_to_all.46 = bf16[4,64,1152]{2,1,0:T(8,128)(2,1)S(1)} all-to-all(bf16[4,64,1152]{2,1,0:T(8,128)(2,1)S(1)} %bitcast.49), channel_id=1, replica_groups=mesh['y'=8,'z'=8,'x'=4,'core'=2] {'x'}, dimensions={0} | all-to-all | bytes 1179648 | tf_op jit(solution)/shard_map/all_to_all | solution.py:318
  345.9 19.7 %all_to_all.47 = bf16[64,2,576]{2,1,0:T(2,128)(2,1)S(1)} all-to-all(bf16[64,2,576]{2,1,0:T(2,128)(2,1)S(1)} %reshape.110), channel_id=1, replica_groups=mesh['y'=8,'z'=8,'x'=4,'core'=2] {'y','z'}, dimensions={0} | all-to-all | bytes 294912 | tf_op jit(solution)/shard_map/all_to_all | solution.py:318
  366.3 1.5 reduce.12
  368.0 15.7 %all_to_all.48 = bf16[64,2,576]{2,1,0:T(2,128)(2,1)S(1)} all-to-all(bf16[64,2,576]{2,1,0:T(2,128)(2,1)S(1)} %reshape.112), channel_id=1, replica_groups=mesh['y'=8,'z'=8,'x'=4,'core'=2] {'y','z'}, dimensions={0} | all-to-all | bytes 294912 | tf_op jit(solution)/shard_map/all_to_all | solution.py:318
  384.0 9.7 %all_to_all.49 = bf16[4,64,1152]{2,1,0:T(8,128)(2,1)S(1)} all-to-all(bf16[4,64,1152]{2,1,0:T(8,128)(2,1)S(1)} %broadcast_in_dim.40), channel_id=1, replica_groups=mesh['y'=8,'z'=8,'x'=4,'core'=2] {'x'}, dimensions={0} | all-to-all | bytes 1179648 | tf_op jit(solution)/shard_map/all_to_all | solution.py:318
  393.7 7.0 %collective-permute-start.1 = (bf16[256,1152]{1,0:T(8,128)(2,1)S(1)}, bf16[256,1152]{1,0:T(8,128)(2,1)S(1)}, u32[]{:S(2)}, u32[]{:S(2)}) collective-permute-start(bf16[256,1152]{1,0:T(8,128)(2,1)S(1)} %bitcast.48), channel_id=1, source_target_pairs={{0,1},{1,0},{2,3},{3,2},{4,5},{5,4},{6,7},{7,6},{8,9},{9,8},{10,11... | collective-permute-start | bytes 1769480 | tf_op jit(solution)/shard_map/ppermute | solution.py:327
  400.7 1.6 collective-permute-done.1
  402.6 1.6 slice_convert_fusion
  (58 shorter events, 11.7 us)
Async XLA Ops:
  12.6 27.9 %all-to-all-start = ((s32[64,1,80]{2,1,0:T(1,128)}), s32[64,1,80]{2,1,0:T(1,128)S(1)}, u32[]{:S(2)}, u32[]{:S(2)}) async-start(s32[64,1,80]{2,1,0:T(1,128)} %bitcast.3), calls=%async_computation | async-start | bytes 65536 | tf_op jit(solution)/shard_map/all_to_all | solution.py:318
  30.7 1.2 copy-start.2
  63.2 6.9 %copy-start.11 = (f32[192,10]{0,1:T(8,128)S(1)}, f32[192,10]{0,1:T(8,128)}, u32[]{:S(2)}) copy-start(f32[192,10]{0,1:T(8,128)} %param.13) | copy-start | bytes 23044
  63.2 153.1 %all-to-all-start.1 = ((bf16[64,80,512]{2,1,0:T(8,128)(2,1)}), bf16[64,80,512]{2,1,0:T(8,128)(2,1)}, u32[]{:S(2)}, u32[]{:S(2)}) async-start(bf16[64,80,512]{2,1,0:T(8,128)(2,1)} %bitcast.43), calls=%async_computation.1 | async-start | bytes 10485760 | tf_op jit(solution)/shard_map/all_to_all | solution.py:318
  69.0 203.9 %all-gather.2.cloned.1.call-start = ((), (), s32[]{:S(2)}) async-start(), calls=%async_computation.8 | async-start | bytes 3194880 | tf_op jit(solution)/shard_map/all_gather | solution.py:343
  216.3 56.6 %copy-start.1 = (bf16[512,1024]{1,0:T(8,128)(2,1)S(1)}, bf16[512,1024]{1,0:T(8,128)(2,1)}, u32[]{:S(2)}) copy-start(bf16[512,1024]{1,0:T(8,128)(2,1)} %q_weight_ref.1) | copy-start | bytes 3145732
  216.3 56.6 %copy-start.8 = (f32[1024]{0:T(1024)S(1)}, f32[1024]{0:T(1024)}, u32[]{:S(2)}) copy-start(f32[1024]{0:T(1024)} %param.15) | copy-start | bytes 12292
  216.3 56.6 %copy-start.9 = (f32[1024]{0:T(1024)S(1)}, f32[1024]{0:T(1024)}, u32[]{:S(2)}) copy-start(f32[1024]{0:T(1024)} %param.17) | copy-start | bytes 12292
  226.8 56.6 %copy-start = (bf16[2112,512]{1,0:T(8,128)(2,1)}, bf16[2112,512]{1,0:T(8,128)(2,1)S(1)}, u32[]{:S(2)}) copy-start(bf16[2112,512]{1,0:T(8,128)(2,1)S(1)} %gather_fusion.1) | copy-start | bytes 6488068
  283.4 16.2 %copy-start.3 = (f32[192,1024]{1,0:T(8,128)}, f32[192,1024]{1,0:T(8,128)S(1)}, u32[]{:S(2)}) copy-start(f32[192,1024]{1,0:T(8,128)S(1)} %get-tuple-element.15.active_ref) | copy-start | bytes 2359300
  283.4 16.2 %copy-start.5 = (f32[192,1024]{1,0:T(8,128)}, f32[192,1024]{1,0:T(8,128)S(1)}, u32[]{:S(2)}) copy-start(f32[192,1024]{1,0:T(8,128)S(1)} %get-tuple-element.16.outer_slope_ref) | copy-start | bytes 2359300
  283.4 23.6 %copy-start.10 = (bf16[1536,1024]{1,0:T(8,128)(2,1)S(1)}, bf16[1536,1024]{1,0:T(8,128)(2,1)}, u32[]{:S(2)}) copy-start(bf16[1536,1024]{1,0:T(8,128)(2,1)} %all-gather.2.cloned.1.call-done.w_ref) | copy-start | bytes 9437188
  299.6 10.2 %collective-permute-start = (bf16[4,128,1152]{2,1,0:T(8,128)(2,1)}, bf16[4,128,1152]{2,1,0:T(8,128)(2,1)}, u32[]{:S(2)}, u32[]{:S(2)}) collective-permute-start(bf16[4,128,1152]{2,1,0:T(8,128)(2,1)} %all_to_all.44), channel_id=1, source_target_pairs={{0,1},{1,0},{2,3},{3,2},{4,5},{5,4},{6,7},{7,6},{8,9},{9,8},{10,11... | collective-permute-start | bytes 3538952 | tf_op jit(solution)/shard_map/ppermute | solution.py:327
  311.7 1.7 copy-start.4
  311.7 1.8 copy-start.6
  311.7 2.2 copy-start.7
  393.7 8.6 %collective-permute-start.1 = (bf16[256,1152]{1,0:T(8,128)(2,1)S(1)}, bf16[256,1152]{1,0:T(8,128)(2,1)S(1)}, u32[]{:S(2)}, u32[]{:S(2)}) collective-permute-start(bf16[256,1152]{1,0:T(8,128)(2,1)S(1)} %bitcast.48), channel_id=1, source_target_pairs={{0,1},{1,0},{2,3},{3,2},{4,5},{5,4},{6,7},{7,6},{8,9},{9,8},{10,11... | collective-permute-start | bytes 1769480 | tf_op jit(solution)/shard_map/ppermute | solution.py:327
Sparse Core Ops, SparseCore 0:
  72.9 199.9 all-gather.1

commit v2 on v1

--- a/solution.py
+++ b/solution.py
@@ -9,7 +9,10 @@
 K = 10
 PAIRS = 64
 NEG_DEV = 64
-SLOTS = 80
+SLOTS = 48
+ALL_SLOTS = 80
+PIECE = 16
+DIGIT = 32
 EXTRA = 128
 
 margin = 0.5
@@ -39,28 +42,79 @@
     return lax.dot_general(a, b, (((0,), (0,)), ((), ())), preferred_element_type=f32)
 
 
-def plan_kernel(owner_ref, local_ref, wanted_ref, place_ref):
+def before(parts):
+    width = parts[0].shape[1]
+    earlier = lax.broadcasted_iota(jnp.int32, (width, width), 0) < lax.broadcasted_iota(
+        jnp.int32, (width, width), 1
+    )
+    inside = jnp.dot(
+        jnp.concatenate([part.astype(bf16) for part in parts], axis=0),
+        earlier.astype(f32).astype(bf16),
+        preferred_element_type=f32,
+    )
+    high = parts[0].shape[0]
+    sums, count = [], jnp.zeros((high, 1), f32)
+    for block, part in enumerate(parts):
+        sums.append(inside[block * high : (block + 1) * high] + count)
+        count = count + jnp.sum(part, axis=1, keepdims=True)
+    return sums, count
+
+
+def pick(wide, values):
+    return jnp.sum(wide * values, axis=0, keepdims=True)
+
+
+def plan_kernel(owner_ref, local_ref, high_ref, low_ref, target_ref, slot_ref):
     blocks, width = owner_ref.shape
-    owners = wanted_ref.shape[0]
-    owner_ids = lax.broadcasted_iota(jnp.int32, (owners, width), 0)
+    owners = high_ref.shape[0]
+    ids = lax.broadcasted_iota(jnp.int32, (owners, width), 0)
+    own = [owner_ref[block : block + 1, :] for block in range(blocks)]
+    local = [local_ref[block : block + 1, :] for block in range(blocks)]
+    first = [(one == ids).astype(f32) for one in own]
+    second = [((one // PIECE) == ids).astype(f32) for one in local]
+    rank, load = before(first)
+    excess = jnp.maximum(load - SLOTS, 0.0)
+    spare = jnp.maximum(SLOTS - load, 0.0)
+    own_excess = [pick(wide, excess) for wide in first]
+    other_spare = [pick(wide, spare) for wide in second]
+    movable = [
+        jnp.where((over > 0.0) & (room > 0.0), 1.0, 0.0)
+        for over, room in zip(own_excess, other_spare)
+    ]
+    queue, _ = before([wide * free for wide, free in zip(second, movable)])
+    queue = [pick(wide, sums) for wide, sums in zip(second, queue)]
+    kept = [
+        jnp.where((free > 0.0) & (place < room), 1.0, 0.0)
+        for free, place, room in zip(movable, queue, other_spare)
+    ]
+    gone, _ = before([wide * free for wide, free in zip(first, kept)])
     slot_ids = lax.broadcasted_iota(jnp.int32, (width, width), 0)
-    earlier = (slot_ids < lax.broadcasted_iota(jnp.int32, (width, width), 1)).astype(f32).astype(bf16)
-    count = jnp.zeros((owners, 1), f32)
     high_sum = jnp.zeros((owners, width), f32)
     low_sum = jnp.zeros((owners, width), f32)
+    widest = jnp.zeros((1, width), jnp.int32)
     for block in range(blocks):
-        own = owner_ref[block : block + 1, :]
-        wide = (own == owner_ids).astype(f32)
-        low_wide = wide.astype(bf16)
-        before = jnp.dot(low_wide, earlier, preferred_element_type=f32) + count
-        slot = jnp.sum(wide * before, axis=0, keepdims=True).astype(jnp.int32)
-        count = count + jnp.sum(wide, axis=1, keepdims=True)
+        gone_before = pick(first[block], gone[block])
+        moved = (kept[block] > 0.0) & (gone_before < own_excess[block])
+        stays = pick(first[block], rank[block]) - jnp.minimum(gone_before, own_excess[block])
+        goes = pick(second[block], load) + queue[block]
+        slot = jnp.where(moved, goes, stays).astype(jnp.int32)
+        row = jnp.where(
+            moved,
+            owners * PIECE + own[block] * PIECE + local[block] % PIECE,
+            local[block],
+        )
+        weight = jnp.where(moved, 1.0, 0.0)
+        wide = (first[block] * (1.0 - weight) + second[block] * weight).astype(bf16)
         there = (slot == slot_ids).astype(f32)
-        local = local_ref[block : block + 1, :]
-        high_sum = high_sum + row_dot(low_wide, (there * (local >> 5).astype(f32)).astype(bf16))
-        low_sum = low_sum + row_dot(low_wide, (there * (local & 31).astype(f32)).astype(bf16))
-        place_ref[block : block + 1, :] = own * SLOTS + slot
-    wanted_ref[...] = (high_sum * 32.0 + low_sum).astype(jnp.int32)
+        high_sum = high_sum + row_dot(wide, (there * (row // DIGIT).astype(f32)).astype(bf16))
+        low_sum = low_sum + row_dot(wide, (there * (row % DIGIT).astype(f32)).astype(bf16))
+        widest = jnp.maximum(widest, slot)
+        target_ref[block : block + 1, :] = jnp.where(moved, local[block] // PIECE, own[block])
+        slot_ref[block : block + 1, :] = slot
+    over = (jnp.max(widest, axis=1, keepdims=True) >= SLOTS).astype(f32)
+    last = lax.broadcasted_iota(jnp.int32, (owners, width), 1) == width - 1
+    high_ref[...] = jnp.where(last, over, high_sum).astype(bf16)
+    low_ref[...] = low_sum.astype(bf16)
 
 
 def plan(owner, local, owners):
@@ -69,16 +123,18 @@
     spare = blocks * 128 - rows
     owner = jnp.pad(owner[:, 0], (0, spare), constant_values=owners).reshape(blocks, 128)
     local = jnp.pad(local[:, 0], (0, spare)).reshape(blocks, 128)
-    wanted, place = pl.pallas_call(
+    high, low, target, slot = pl.pallas_call(
         plan_kernel,
         out_shape=(
-            jax.ShapeDtypeStruct((owners, 128), jnp.int32),
+            jax.ShapeDtypeStruct((owners, 128), bf16),
+            jax.ShapeDtypeStruct((owners, 128), bf16),
+            jax.ShapeDtypeStruct((blocks, 128), jnp.int32),
             jax.ShapeDtypeStruct((blocks, 128), jnp.int32),
         ),
         compiler_params=params(),
         name="plan",
     )(owner, local)
-    return wanted[:, :SLOTS], place.reshape(-1)[:rows]
+    return high, low, target.reshape(-1)[:rows], slot.reshape(-1)[:rows]
 
 
 def dequantize_kernel(slab_ref, scales_ref, out_ref):
@@ -96,6 +152,12 @@
 def column(values, at):
     lanes = lax.broadcasted_iota(jnp.int32, values.shape, 1)
     return jnp.sum(jnp.where(lanes == at, values, 0.0), axis=1, keepdims=True)
+
+
+def columns(w_ref, part, start, end):
+    return jnp.concatenate(
+        [w_ref[2 * part, start:end, :], w_ref[2 * part + 1, start:end, :]], axis=1
+    )
 
 
 def forward_kernel(
@@ -133,11 +195,15 @@
     def _():
         width = own_ref.shape[1]
         hidden = active_ref.shape[1]
-        outer = (
-            jnp.dot(own_ref[...], w_ref[:width, :], preferred_element_type=f32)
-            + jnp.dot(pooled[...].astype(bf16), w_ref[width:, :], preferred_element_type=f32)
-            + w_bias_ref[...]
+        joined = jnp.concatenate([own_ref[...], pooled[...].astype(bf16)], axis=1)
+        outer = jnp.concatenate(
+            [
+                jnp.dot(joined, columns(w_ref, part, 0, width + hidden), preferred_element_type=f32)
+                for part in range(w_ref.shape[0] // 2)
+            ],
+            axis=1,
         )
+        outer = outer + w_bias_ref[...]
         gate = sigmoid(outer)
         active = outer * gate
         active_ref[...] = active
@@ -258,7 +324,13 @@
         along = jnp.sum(d_embed * active, axis=1, keepdims=True)
         d_active = scaling * (d_embed - active * (along * scaling * scaling / hidden))
         d_outer = (d_active * outer_slope_ref[...]).astype(bf16)
-        d_pooled[...] = row_dot(d_outer, w_ref[...])
+        width = fetched_ref.shape[1]
+        pair = 2 * w_ref.shape[2]
+        sums = jnp.zeros((targets, hidden), f32)
+        for part in range(w_ref.shape[0] // 2):
+            lanes = slice(part * pair, (part + 1) * pair)
+            sums = sums + row_dot(d_outer[:, lanes], columns(w_ref, part, width, width + hidden))
+        d_pooled[...] = sums
         bias_sum[...] = jnp.zeros_like(bias_sum)
 
     share = column(shares_of(importance_ref[...]), step)
@@ -294,7 +366,7 @@
         in_specs=[
             whole(fetched.shape),
             whole(importance.shape),
-            whole((hidden, hidden)),
+            whole(w_full.shape),
             pl.BlockSpec((targets, hidden), lambda step: (step, 0)),
             whole(embedded.shape),
             whole(active.shape),
@@ -311,7 +383,7 @@
         ],
         compiler_params=params(),
         name="backward",
-    )(fetched, importance, w_full[width:], slope, embedded, active, outer_slope, group)
+    )(fetched, importance, w_full, slope, embedded, active, outer_slope, group)
 
 
 def exchange(values, axes):
@@ -321,12 +393,6 @@
 def spread(values, axes):
     count = lax.axis_size(axes)
     return exchange(jnp.broadcast_to(values[None], (count,) + values.shape), axes)
-
-
-def both_cores(values):
-    other = lax.ppermute(values, "core", [(0, 1), (1, 0)])
-    first = lax.axis_index("core") == 0
-    return jnp.stack([jnp.where(first, values, other), jnp.where(first, other, values)])
 
 
 def total(values, axes):
@@ -340,23 +406,59 @@
     pin_count = lax.axis_size(PIN)
     targets = importance.shape[0]
     width, hidden = q_weight.shape
-    w_full = lax.all_gather(w_weight, PIN, axis=0, tiled=True)
-    wanted, place = plan(owner, local, pin_count)
+    high, low, target, slot = plan(owner, local, pin_count)
     ready = pl.pallas_call(
         dequantize_kernel,
         out_shape=jax.ShapeDtypeStruct(slab.shape, bf16),
         compiler_params=params(),
         name="dequantize",
     )(slab, scales)
-    asked = exchange(wanted, PIN)
-    picked = jnp.take(ready, asked.reshape(-1), axis=0, mode="clip")
+    members = lax.axis_size(GRP)
+    lanes = hidden // members
+    rows = w_weight.shape[0]
+    mine = lax.dynamic_slice_in_dim(w_weight, lax.axis_index(GRP) * lanes, lanes, 1)
+    mine = mine.reshape(rows // 8, 8, lanes).transpose(1, 0, 2).reshape(8, -1)
+    ids = jnp.concatenate([high[:, None], low[:, None]], axis=1)
+    tail = jnp.concatenate(
+        [
+            jnp.broadcast_to(mine[None], (pin_count,) + mine.shape),
+            jnp.pad(ids, ((0, 0), (0, 6), (0, 0))),
+        ],
+        axis=2,
+    )
+    sent = jnp.concatenate([ready.reshape(pin_count, PIECE, width), tail], axis=1)
+    sent = exchange(sent, PIN)
+    table = jnp.concatenate([ready, sent[:, :PIECE].reshape(pin_count * PIECE, width)], axis=0)
+    ids = sent[:, PIECE : PIECE + 2, mine.shape[1] :].astype(jnp.int32)
+    asked = ids[:, 0, :ALL_SLOTS] * DIGIT + ids[:, 1, :ALL_SLOTS]
+    picked = jnp.take(table, asked[:, :SLOTS].reshape(-1), axis=0, mode="clip")
     got = exchange(picked.reshape(pin_count, SLOTS, width), PIN).reshape(-1, width)
-    by_neighbour = place.reshape(targets, K + 1).T.reshape(-1)
-    fetched = jnp.take(got, by_neighbour, axis=0, mode="clip")
+    w_part = sent[:, PIECE:, : mine.shape[1]].reshape(pin_count, 8, rows // 8, lanes)
+    w_part = w_part.transpose(0, 2, 1, 3).reshape(pin_count * rows, lanes)
+    over = jnp.max(sent[:, PIECE, -1])
+    w_part = jnp.concatenate([w_part, jnp.broadcast_to(over, (16, lanes))], axis=0)
+    w_full = lax.all_gather(w_part, GRP, axis=0, tiled=False)
+    over = jnp.max(w_full[:, -16:, :].astype(f32)) > 0.5
+
+    def ordered(values):
+        return values.reshape(targets, K + 1).T.reshape(-1)
+
+    target, slot = ordered(target), ordered(slot)
+    late = slot >= SLOTS
+    fetched = jnp.take(got, jnp.where(late, 0, target * SLOTS + slot), axis=0, mode="clip")
+
+    def second_exchange(fetched):
+        more = ALL_SLOTS - SLOTS
+        picked = jnp.take(table, asked[:, SLOTS:].reshape(-1), axis=0, mode="clip")
+        got = exchange(picked.reshape(pin_count, more, width), PIN).reshape(-1, width)
+        place = jnp.where(late, target * more + slot - SLOTS, 0)
+        return jnp.where(late[:, None], jnp.take(got, place, axis=0, mode="clip"), fetched)
+
+    fetched = lax.cond(over, second_exchange, lambda fetched: fetched, fetched)
     slope, embedded, active, outer_slope, payload = forward(
         fetched, importance, q_weight, q_bias, w_full, w_bias
     )
-    group = both_cores(spread(payload, "x"))
+    group = spread(spread(payload, "x"), "core")
     group = group.reshape((-1,) + payload.shape)
     grads = backward(fetched, importance, w_full, slope, embedded, active, outer_slope, group)
     grads = total(grads, "core").astype(bf16)
@@ -366,7 +468,7 @@
     split = grads.astype(bf16)
     grads = spread(split, PIN).reshape(-1, hidden + EXTRA)
     grads = spread(grads, "x").reshape(-1, hidden + EXTRA)
-    grads = both_cores(grads).reshape(-1, hidden + EXTRA)
+    grads = spread(grads, "core").reshape(-1, hidden + EXTRA)
     grad_q = grads[:, :hidden].astype(f32)
     grad_bias = grads[:loss_row, hidden:].astype(f32).reshape(-1)
     objective = jnp.sum(grads[loss_row : loss_row + 2, hidden].astype(f32))

time: 415 us -> 336 us (0.81)
  waiting for transfers between devices: 205 us -> 68.9 us
  blocking collectives: 78.1 us -> 169 us
  starting transfers between devices: 37.4 us -> 10.3 us
  local copies, waits for them, and re-layouts: 37.4 us -> 32.2 us
    all_to_all x2 -> x1, waiting for transfers between devices: 154 us -> 33.4 us  [exchange(): return lax.all_to_all(values, axes, split_axis=0, concat_axis=0, tiled=True)]
    all_to_all x6 -> x9, blocking collectives: 78.1 us -> 169 us  [exchange(): return lax.all_to_all(values, axes, split_axis=0, concat_axis=0, tiled=True)]
    ppermute x2 -> x0, starting transfers between devices: 14.4 us -> none  [both_cores(): other = lax.ppermute(values, 'core', [(0, 1), (1, 0)])]
    all_to_all x2 -> x1, starting transfers between devices: 22.9 us -> 10.3 us  [exchange(): return lax.all_to_all(values, axes, split_axis=0, concat_axis=0, tiled=True)]
    gather x2, local copies, waits for them, and re-layouts: 31.8 us -> 20.7 us  [the longest x1 13.2 us: body(): picked = jnp.take(table, asked[:, :SLOTS].reshape(-1), axis=0, mode='clip')]
    all_gather x1, waiting for transfers between devices: 46.1 us -> 35.4 us  [body(): w_full = lax.all_gather(w_part, GRP, axis=0, tiled=False)]
    ppermute x2 -> x0, waiting for transfers between devices: 4.21 us -> none  [both_cores(): other = lax.ppermute(values, 'core', [(0, 1), (1, 0)])]
  transfers between devices with their start and end apart: 5 -> 2, of which waited for: 5 -> 2; matrix products, arithmetic and copies ran while one was open for 3% -> 2% of each run, Pallas kernels for 0% -> 0%
where the time goes in v2:
time: 336 us; the launch traced here: 334 us
  blocking collectives  169 us (50%)
  waiting for transfers between devices  68.9 us (21%)
  local copies, waits for them, and re-layouts  32.2 us (10%)
  Pallas kernels  26.7 us (8%)
  between operations  16.8 us (5%)
  other arithmetic  10.6 us (3%)
  starting transfers between devices  10.3 us (3%)
    all_to_all x9, blocking collectives, exchange(): return lax.all_to_all(values, axes, split_axis=0, concat_axis=0, tiled=True)  169 us
    all_gather x1, waiting for transfers between devices, body(): w_full = lax.all_gather(w_part, GRP, axis=0, tiled=False)  35.4 us
    all_to_all x1, waiting for transfers between devices, exchange(): return lax.all_to_all(values, axes, split_axis=0, concat_axis=0, tiled=True)  33.4 us
    pallas_call x1, Pallas kernels, backward(): pl.pallas_call(backward_kernel, grid=(K,), in_specs=[whole(fetched.shape)...  13.6 us
    gather x1, local copies, waits for them, and re-layouts, body(): picked = jnp.take(table, asked[:, :SLOTS].reshape(-1), axis=0, mode='clip')  13.2 us
    pallas_call x1, Pallas kernels, forward(): pl.pallas_call(forward_kernel, grid=(K,), in_specs=[pl.BlockSpec((targets...  11 us
    all_to_all x1, starting transfers between devices, exchange(): return lax.all_to_all(values, axes, split_axis=0, concat_axis=0, tiled=True)  10.3 us
    gather x1, local copies, waits for them, and re-layouts, body(): jnp.take(got, jnp.where(late, 0, target * SLOTS + slot), axis=0, mode='cl...  7.43 us
  transfers between devices with their start and end apart: 2, of which 2 were waited for; matrix products, arithmetic and copies ran while one was open for 2% of the time, Pallas kernels for 0%

profile of v2, /device:TPU:1, one launch (start us, length us, event | category | flops | bytes accessed | tf_op | source)
XLA Modules:
  0.0 334.5 jit_solution(15470622673413495071)
XLA Ops:
  8.7 1.7 plan.1
  13.3 54.5 %all_to_all.54 = bf16[64,24,512]{2,1,0:T(8,128)(2,1)S(1)} all-to-all(bf16[64,24,512]{2,1,0:T(8,128)(2,1)S(1)} %fusion.4), channel_id=1, replica_groups=mesh['y'=8,'z'=8,'x'=4,'core'=2] {'y','z'}, dimensions={0} | all-to-all | bytes 3145728 | tf_op jit(solution)/shard_map/all_to_all | solution.py:390
  69.2 13.2 %gather_fusion.2 = bf16[3072,512]{1,0:T(8,128)(2,1)} fusion(bf16[2048,512]{1,0:T(8,128)(2,1)S(1)} %pad_maximum_fusion, s32[3072]{0:T(1024)S(1)} %broadcast_clamp_fusion.1), kind=kCustom, calls=%fused_computation.2 | custom fusion | bytes 6303744 | tf_op jit(solution)/shard_map/jit(_take)/gather | solution.py:434
  82.4 10.3 %all-to-all-start.2 = ((bf16[64,48,512]{2,1,0:T(8,128)(2,1)}), bf16[64,48,512]{2,1,0:T(8,128)(2,1)S(1)}, u32[]{:S(2)}, u32[]{:S(2)}) async-start(bf16[64,48,512]{2,1,0:T(8,128)(2,1)} %bitcast.63), calls=%async_computation.2 | async-start | bytes 6291456 | tf_op jit(solution)/shard_map/all_to_all | solution.py:390
  93.8 1.6 slice_reduce_fusion.1
  95.5 1.4 concatenate.18
  97.6 35.4 %all-gather.3.cloned.1.call-done = bf16[12416,128]{1,0:T(8,128)(2,1)} async-done(((bf16[1552,128]{1,0:T(8,128)(2,1)}), bf16[12416,128]{1,0:T(8,128)(2,1)}) %all-gather.3.cloned.1.call-update) | async-done | bytes 3178512 | tf_op jit(solution)/shard_map/all_gather | solution.py:440
  133.1 1.4 slice_reduce_fusion
  135.1 33.4 %all-to-all-done.2 = bf16[64,48,512]{2,1,0:T(8,128)(2,1)S(1)} async-done(((bf16[64,48,512]{2,1,0:T(8,128)(2,1)}), bf16[64,48,512]{2,1,0:T(8,128)(2,1)S(1)}, u32[]{:S(2)}, u32[]{:S(2)}) %all-to-all-start.2) | async-done | bytes 3145760 | tf_op jit(solution)/shard_map/all_to_all | solution.py:390
  168.5 7.4 %gather_fusion.3 = bf16[2112,512]{1,0:T(8,128)(2,1)} fusion(bf16[3072,512]{1,0:T(8,128)(2,1)S(1)} %bitcast.62, s32[3072]{0:T(1024)S(1)} %pad_clamp_fusion.1), kind=kCustom, calls=%fused_computation.3 | custom fusion | bytes 4333824 | tf_op jit(solution)/shard_map/jit(_take)/gather | solution.py:448
  176.0 1.9 copy-done.1
  177.9 1.2 copy-done.2
  179.1 11.0 %forward.1 = (bf16[1920,1024]{1,0:T(8,128)(2,1)}, bf16[192,1024]{1,0:T(8,128)(2,1)}, f32[192,1024]{1,0:T(8,128)S(1)}, f32[192,1024]{1,0:T(8,128)S(1)}, bf16[128,1152]{1,0:T(8,128)(2,1)S(1)}) custom-call(bf16[2112,512]{1,0:T(8,128)(2,1)} %get-tuple-element.74.own_ref.near_ref.fetched_ref, bf16[2112,512]{1,0:T(8,128)(2,1)} %get-tuple-element.74.own_ref.near_ref.fetched_ref, ...), custom_call_target="tpu_custom_call" | custom-call | tf_op jit(solution)/shard_map/forward/pallas_call | solution.py:238
  190.2 15.0 %all_to_all.55 = bf16[4,128,1152]{2,1,0:T(8,128)(2,1)S(1)} all-to-all(bf16[4,128,1152]{2,1,0:T(8,128)(2,1)S(1)} %broadcast_in_dim.89), channel_id=1, replica_groups=mesh['y'=8,'z'=8,'x'=4,'core'=2] {'x'}, dimensions={0} | all-to-all | bytes 2359296 | tf_op jit(solution)/shard_map/all_to_all | solution.py:390
  205.5 11.3 %all_to_all.56 = bf16[2,4,128,1152]{3,2,1,0:T(8,128)(2,1)S(1)} all-to-all(bf16[2,4,128,1152]{3,2,1,0:T(8,128)(2,1)S(1)} %broadcast_in_dim.90), channel_id=1, replica_groups=mesh['y'=8,'z'=8,'x'=4,'core'=2] {'core'}, dimensions={0} | all-to-all | bytes 4718592 | tf_op jit(solution)/shard_map/all_to_all | solution.py:390
  216.9 13.6 %backward.1 = bf16[512,1152]{1,0:T(8,128)(2,1)S(1)} custom-call(bf16[2112,512]{1,0:T(8,128)(2,1)S(1)} %copy-done.8, f32[192,10]{1,0:T(8,128)S(1)} %copy.52.importance_ref, bf16[8,1552,128]{2,1,0:T(8,128)(2,1)} %bitcast.51, bf16[1920,1024]{1,0:T(8,128)(2,1)} %get-tuple-element.43.slope_ref, bf16[192,1024]{1,0:T(8,128)(2,1)S(1)} %copy-done.4, ...), custom_call_target="tpu_custom_call" | custom-call | tf_op jit(solution)/shard_map/backward/pallas_call | solution.py:363
  230.5 4.7 %all_to_all.57 = bf16[2,256,1152]{2,1,0:T(8,128)(2,1)S(1)} all-to-all(bf16[2,256,1152]{2,1,0:T(8,128)(2,1)S(1)} %bitcast.55), channel_id=1, replica_groups=mesh['y'=8,'z'=8,'x'=4,'core'=2] {'core'}, dimensions={0} | all-to-all | bytes 2359296 | tf_op jit(solution)/shard_map/all_to_all | solution.py:390
  235.4 12.0 %all_to_all.58 = bf16[4,64,1152]{2,1,0:T(8,128)(2,1)S(1)} all-to-all(bf16[4,64,1152]{2,1,0:T(8,128)(2,1)S(1)} %bitcast.70), channel_id=1, replica_groups=mesh['y'=8,'z'=8,'x'=4,'core'=2] {'x'}, dimensions={0} | all-to-all | bytes 1179648 | tf_op jit(solution)/shard_map/all_to_all | solution.py:390
  248.9 36.6 %all_to_all.59 = bf16[64,2,576]{2,1,0:T(2,128)(2,1)S(1)} all-to-all(bf16[64,2,576]{2,1,0:T(2,128)(2,1)S(1)} %reshape.222), channel_id=1, replica_groups=mesh['y'=8,'z'=8,'x'=4,'core'=2] {'y','z'}, dimensions={0} | all-to-all | bytes 294912 | tf_op jit(solution)/shard_map/all_to_all | solution.py:390
  286.2 1.5 reduce.10
  287.9 15.7 %all_to_all.60 = bf16[64,2,576]{2,1,0:T(2,128)(2,1)S(1)} all-to-all(bf16[64,2,576]{2,1,0:T(2,128)(2,1)S(1)} %reshape.224), channel_id=1, replica_groups=mesh['y'=8,'z'=8,'x'=4,'core'=2] {'y','z'}, dimensions={0} | all-to-all | bytes 294912 | tf_op jit(solution)/shard_map/all_to_all | solution.py:390
  303.9 9.7 %all_to_all.61 = bf16[4,64,1152]{2,1,0:T(8,128)(2,1)S(1)} all-to-all(bf16[4,64,1152]{2,1,0:T(8,128)(2,1)S(1)} %broadcast_in_dim.93), channel_id=1, replica_groups=mesh['y'=8,'z'=8,'x'=4,'core'=2] {'x'}, dimensions={0} | all-to-all | bytes 1179648 | tf_op jit(solution)/shard_map/all_to_all | solution.py:390
  313.7 9.4 %all_to_all.62 = bf16[2,256,1152]{2,1,0:T(8,128)(2,1)S(1)} all-to-all(bf16[2,256,1152]{2,1,0:T(8,128)(2,1)S(1)} %broadcast_in_dim.95), channel_id=1, replica_groups=mesh['y'=8,'z'=8,'x'=4,'core'=2] {'core'}, dimensions={0} | all-to-all | bytes 2359296 | tf_op jit(solution)/shard_map/all_to_all | solution.py:390
  323.1 1.6 slice_convert_fusion
  (66 shorter events, 12.0 us)
Async XLA Ops:
  7.2 5.9 %copy-start = (bf16[24,1024]{1,0:T(8,128)(2,1)S(1)}, bf16[24,1024]{1,0:T(8,128)(2,1)}, u32[]{:S(2)}) copy-start(bf16[24,1024]{1,0:T(8,128)(2,1)} %param.18) | copy-start | bytes 147460
  11.4 1.2 copy-start.3
  67.8 1.2 copy-start.9
  69.0 13.4 %copy-start.7 = (bf16[2048,512]{1,0:T(8,128)(2,1)}, bf16[2048,512]{1,0:T(8,128)(2,1)S(1)}, u32[]{:S(2)}) copy-start(bf16[2048,512]{1,0:T(8,128)(2,1)S(1)} %pad_maximum_fusion) | copy-start | bytes 6291460
  69.1 13.3 %copy-start.10 = (s32[64,1,80]{2,1,0:T(1,128)}, s32[64,1,80]{2,1,0:T(1,128)S(1)}, u32[]{:S(2)}) copy-start(s32[64,1,80]{2,1,0:T(1,128)S(1)} %slice_add_fusion) | copy-start | bytes 61444
  82.4 86.1 %all-to-all-start.2 = ((bf16[64,48,512]{2,1,0:T(8,128)(2,1)}), bf16[64,48,512]{2,1,0:T(8,128)(2,1)S(1)}, u32[]{:S(2)}, u32[]{:S(2)}) async-start(bf16[64,48,512]{2,1,0:T(8,128)(2,1)} %bitcast.63), calls=%async_computation.2 | async-start | bytes 6291456 | tf_op jit(solution)/shard_map/all_to_all | solution.py:390
  92.7 4.8 %copy-start.11 = (f32[192,10]{0,1:T(8,128)S(1)}, f32[192,10]{0,1:T(8,128)}, u32[]{:S(2)}) copy-start(f32[192,10]{0,1:T(8,128)} %param.15) | copy-start | bytes 23044
  92.7 40.4 %all-gather.3.cloned.1.call-start = ((), (), s32[]{:S(2)}) async-start(), calls=%async_computation.11 | async-start | bytes 3575808 | tf_op jit(solution)/shard_map/all_gather | solution.py:440
  176.0 1.9 copy-start.1
  176.0 1.9 copy-start.5
  176.0 1.9 copy-start.6
  177.9 1.2 copy-start.2
  205.5 11.4 %copy-start.4 = (bf16[192,1024]{1,0:T(8,128)(2,1)S(1)}, bf16[192,1024]{1,0:T(8,128)(2,1)}, u32[]{:S(2)}) copy-start(bf16[192,1024]{1,0:T(8,128)(2,1)} %get-tuple-element.34.embedded_ref) | copy-start | bytes 1179652
  205.5 11.4 %copy-start.8 = (bf16[2112,512]{1,0:T(8,128)(2,1)S(1)}, bf16[2112,512]{1,0:T(8,128)(2,1)}, u32[]{:S(2)}) copy-start(bf16[2112,512]{1,0:T(8,128)(2,1)} %get-tuple-element.74.own_ref.near_ref.fetched_ref) | copy-start | bytes 6488068
Sparse Core Ops, SparseCore 0:
  97.0 35.9 all-gather.2

commit v3 on v2

--- a/solution.py
+++ b/solution.py
@@ -9,9 +9,11 @@
 K = 10
 PAIRS = 64
 NEG_DEV = 64
-SLOTS = 48
+SLOTS = 40
 ALL_SLOTS = 80
 PIECE = 16
+COPIED = 12
+TARGETS = (44, 36, 40, 40)
 DIGIT = 32
 EXTRA = 128
 
@@ -57,7 +59,7 @@
     for block, part in enumerate(parts):
         sums.append(inside[block * high : (block + 1) * high] + count)
         count = count + jnp.sum(part, axis=1, keepdims=True)
-    return sums, count
+    return sums
 
 
 def pick(wide, values):
@@ -72,48 +74,56 @@
     local = [local_ref[block : block + 1, :] for block in range(blocks)]
     first = [(one == ids).astype(f32) for one in own]
     second = [((one // PIECE) == ids).astype(f32) for one in local]
-    rank, load = before(first)
-    excess = jnp.maximum(load - SLOTS, 0.0)
-    spare = jnp.maximum(SLOTS - load, 0.0)
-    own_excess = [pick(wide, excess) for wide in first]
-    other_spare = [pick(wide, spare) for wide in second]
-    movable = [
-        jnp.where((over > 0.0) & (room > 0.0), 1.0, 0.0)
-        for over, room in zip(own_excess, other_spare)
-    ]
-    queue, _ = before([wide * free for wide, free in zip(second, movable)])
-    queue = [pick(wide, sums) for wide, sums in zip(second, queue)]
-    kept = [
-        jnp.where((free > 0.0) & (place < room), 1.0, 0.0)
-        for free, place, room in zip(movable, queue, other_spare)
-    ]
-    gone, _ = before([wide * free for wide, free in zip(first, kept)])
+    free = [jnp.where(one % PIECE < COPIED, 1.0, 0.0) for one in local]
+    moved = [jnp.zeros((1, width), f32)] * blocks
+    load = sum(jnp.sum(wide, axis=1, keepdims=True) for wide in first)
+    for goal in TARGETS:
+        excess = jnp.maximum(load - goal, 0.0)
+        spare = jnp.maximum(goal - load, 0.0)
+        over = [pick(wide, excess) for wide in first]
+        room = [pick(wide, spare) for wide in second]
+        movable = [
+            jnp.where((most > 0.0) & (least > 0.0), one, 0.0)
+            for most, least, one in zip(over, room, free)
+        ]
+        queue = before([wide * one for wide, one in zip(second, movable)])
+        kept = [
+            jnp.where(pick(wide, sums) < least, one, 0.0)
+            for wide, sums, least, one in zip(second, queue, room, movable)
+        ]
+        gone = before([wide * one for wide, one in zip(first, kept)])
+        new = [
+            jnp.where(pick(wide, sums) < most, one, 0.0)
+            for wide, sums, most, one in zip(first, gone, over, kept)
+        ]
+        moved = [one + more for one, more in zip(moved, new)]
+        free = [one - more for one, more in zip(free, new)]
+        change = sum((there - here) * more for here, there, more in zip(first, second, new))
+        load = load + jnp.sum(change, axis=1, keepdims=True)
+    holder = [here + (there - here) * one for here, there, one in zip(first, second, moved)]
+    rank = before(holder)
     slot_ids = lax.broadcasted_iota(jnp.int32, (width, width), 0)
     high_sum = jnp.zeros((owners, width), f32)
     low_sum = jnp.zeros((owners, width), f32)
     widest = jnp.zeros((1, width), jnp.int32)
     for block in range(blocks):
-        gone_before = pick(first[block], gone[block])
-        moved = (kept[block] > 0.0) & (gone_before < own_excess[block])
-        stays = pick(first[block], rank[block]) - jnp.minimum(gone_before, own_excess[block])
-        goes = pick(second[block], load) + queue[block]
-        slot = jnp.where(moved, goes, stays).astype(jnp.int32)
+        slot = pick(holder[block], rank[block]).astype(jnp.int32)
+        other = moved[block] > 0.0
         row = jnp.where(
-            moved,
+            other,
             owners * PIECE + own[block] * PIECE + local[block] % PIECE,
             local[block],
         )
-        weight = jnp.where(moved, 1.0, 0.0)
-        wide = (first[block] * (1.0 - weight) + second[block] * weight).astype(bf16)
+        wide = holder[block].astype(bf16)
         there = (slot == slot_ids).astype(f32)
         high_sum = high_sum + row_dot(wide, (there * (row // DIGIT).astype(f32)).astype(bf16))
         low_sum = low_sum + row_dot(wide, (there * (row % DIGIT).astype(f32)).astype(bf16))
         widest = jnp.maximum(widest, slot)
-        target_ref[block : block + 1, :] = jnp.where(moved, local[block] // PIECE, own[block])
+        target_ref[block : block + 1, :] = jnp.where(other, local[block] // PIECE, own[block])
         slot_ref[block : block + 1, :] = slot
-    over = (jnp.max(widest, axis=1, keepdims=True) >= SLOTS).astype(f32)
+    late = (jnp.max(widest, axis=1, keepdims=True) >= SLOTS).astype(f32)
     last = lax.broadcasted_iota(jnp.int32, (owners, width), 1) == width - 1
-    high_ref[...] = jnp.where(last, over, high_sum).astype(bf16)
+    high_ref[...] = jnp.where(last, late, high_sum).astype(bf16)
     low_ref[...] = low_sum.astype(bf16)
 
 
@@ -166,7 +176,7 @@
     importance_ref,
     q_weight_ref,
     q_bias_ref,
-    w_ref,
+    w_far_ref,
     w_bias_ref,
     slope_ref,
     embedded_ref,
@@ -174,8 +184,16 @@
     outer_slope_ref,
     payload_ref,
     pooled,
+    w_ref,
+    w_arrived,
 ):
     step = pl.program_id(0)
+    w_copy = pltpu.make_async_copy(w_far_ref, w_ref, w_arrived)
+
+    @pl.when(step == 0)
+    def _():
+        w_copy.start()
+
     share = column(shares_of(importance_ref[...]), step)
     inner = jnp.dot(near_ref[...], q_weight_ref[...], preferred_element_type=f32) + q_bias_ref[...]
     gate = sigmoid(inner)
@@ -193,6 +211,7 @@
 
     @pl.when(step == pl.num_programs(0) - 1)
     def _():
+        w_copy.wait()
         width = own_ref.shape[1]
         hidden = active_ref.shape[1]
         joined = jnp.concatenate([own_ref[...], pooled[...].astype(bf16)], axis=1)
@@ -244,7 +263,7 @@
             whole(importance.shape),
             whole(q_weight.shape),
             whole((1, hidden)),
-            whole(w_full.shape),
+            pl.BlockSpec(memory_space=pl.ANY),
             whole((1, hidden)),
         ],
         out_specs=[
@@ -261,7 +280,11 @@
             jax.ShapeDtypeStruct((targets, hidden), f32),
             jax.ShapeDtypeStruct((sent, hidden + EXTRA), bf16),
         ),
-        scratch_shapes=[pltpu.VMEM((targets, hidden), f32)],
+        scratch_shapes=[
+            pltpu.VMEM((targets, hidden), f32),
+            pltpu.VMEM(w_full.shape, bf16),
+            pltpu.SemaphoreType.DMA,
+        ],
         compiler_params=params(),
         name="forward",
     )(fetched, fetched, importance, q_weight, q_bias[None, :], w_full, w_bias[None, :])
@@ -417,25 +440,22 @@
     lanes = hidden // members
     rows = w_weight.shape[0]
     mine = lax.dynamic_slice_in_dim(w_weight, lax.axis_index(GRP) * lanes, lanes, 1)
-    mine = mine.reshape(rows // 8, 8, lanes).transpose(1, 0, 2).reshape(8, -1)
-    ids = jnp.concatenate([high[:, None], low[:, None]], axis=1)
-    tail = jnp.concatenate(
-        [
-            jnp.broadcast_to(mine[None], (pin_count,) + mine.shape),
-            jnp.pad(ids, ((0, 0), (0, 6), (0, 0))),
-        ],
-        axis=2,
-    )
-    sent = jnp.concatenate([ready.reshape(pin_count, PIECE, width), tail], axis=1)
-    sent = exchange(sent, PIN)
-    table = jnp.concatenate([ready, sent[:, :PIECE].reshape(pin_count * PIECE, width)], axis=0)
-    ids = sent[:, PIECE : PIECE + 2, mine.shape[1] :].astype(jnp.int32)
-    asked = ids[:, 0, :ALL_SLOTS] * DIGIT + ids[:, 1, :ALL_SLOTS]
+    tail = jnp.broadcast_to(mine[PIECE:].reshape(1, 2, width), (pin_count, 2, width))
+    ids = jnp.pad(jnp.concatenate([high, low], axis=1), ((0, 0), (0, width - 256)))
+    tail = jnp.concatenate([tail, jnp.pad(ids[:, None], ((0, 0), (0, 1), (0, 0)))], axis=1)
+    sent = jnp.concatenate([ready.reshape(pin_count, PIECE, width)[:, :COPIED], tail], axis=1)
+    side = jnp.broadcast_to(mine[None, :PIECE], (pin_count, PIECE, lanes))
+    sent = exchange(jnp.concatenate([sent, side], axis=2), PIN)
+    table = sent[:, :, :width].reshape(pin_count * PIECE, width)
+    table = jnp.concatenate([ready, table], axis=0)
+    ids = sent[:, COPIED + 2].astype(jnp.int32)
+    asked = ids[:, :ALL_SLOTS] * DIGIT + ids[:, 128 : 128 + ALL_SLOTS]
     picked = jnp.take(table, asked[:, :SLOTS].reshape(-1), axis=0, mode="clip")
     got = exchange(picked.reshape(pin_count, SLOTS, width), PIN).reshape(-1, width)
-    w_part = sent[:, PIECE:, : mine.shape[1]].reshape(pin_count, 8, rows // 8, lanes)
-    w_part = w_part.transpose(0, 2, 1, 3).reshape(pin_count * rows, lanes)
-    over = jnp.max(sent[:, PIECE, -1])
+    w_part = sent[:, COPIED : COPIED + 2, :width].reshape(pin_count, rows - PIECE, lanes)
+    w_part = jnp.concatenate([sent[:, :, width:], w_part], axis=1)
+    w_part = w_part.reshape(pin_count * rows, lanes)
+    over = jnp.max(sent[:, COPIED + 2, 127])
     w_part = jnp.concatenate([w_part, jnp.broadcast_to(over, (16, lanes))], axis=0)
     w_full = lax.all_gather(w_part, GRP, axis=0, tiled=False)
     over = jnp.max(w_full[:, -16:, :].astype(f32)) > 0.5
@@ -462,12 +482,10 @@
     group = group.reshape((-1,) + payload.shape)
     grads = backward(fetched, importance, w_full, slope, embedded, active, outer_slope, group)
     grads = total(grads, "core").astype(bf16)
-    grads = total(grads, "x").astype(bf16)
     grads = total(grads, PIN)
+    grads = jnp.sum(spread(grads, "x"), axis=0)
     loss_row = hidden // EXTRA
-    split = grads.astype(bf16)
-    grads = spread(split, PIN).reshape(-1, hidden + EXTRA)
-    grads = spread(grads, "x").reshape(-1, hidden + EXTRA)
+    grads = spread(grads.astype(bf16), PIN).reshape(-1, hidden + EXTRA)
     grads = spread(grads, "core").reshape(-1, hidden + EXTRA)
     grad_q = grads[:, :hidden].astype(f32)
     grad_bias = grads[:loss_row, hidden:].astype(f32).reshape(-1)

time: 336 us -> 309 us (0.920)
  waiting for transfers between devices: 68.9 us -> 58.9 us
  blocking collectives: 169 us -> 160 us
  local copies, waits for them, and re-layouts: 32.2 us -> 25.7 us
    all_gather x1, waiting for transfers between devices: 35.4 us -> 0.01 us  [body(): w_full = lax.all_gather(w_part, GRP, axis=0, tiled=False)]
    all_to_all x1, waiting for transfers between devices: 33.4 us -> 58.9 us  [exchange(): return lax.all_to_all(values, axes, split_axis=0, concat_axis=0, tiled=True)]
    all_to_all x9 -> x8, blocking collectives: 169 us -> 160 us  [exchange(): return lax.all_to_all(values, axes, split_axis=0, concat_axis=0, tiled=True)]
    gather x1, local copies, waits for them, and re-layouts: 13.2 us -> 8.2 us  [body(): picked = jnp.take(table, asked[:, :SLOTS].reshape(-1), axis=0, mode='clip')]
    unnamed x32 -> x22, local copies, waits for them, and re-layouts: 7.14 us -> 5.28 us
  transfers between devices with their start and end apart: 2 -> 2, of which waited for: 2 -> 1; matrix products, arithmetic and copies ran while one was open for 2% -> 5% of each run, Pallas kernels for 0% -> 0%
where the time goes in v3:
time: 309 us; the launch traced here: 308 us
  blocking collectives  160 us (52%)
  waiting for transfers between devices  58.9 us (19%)
  Pallas kernels  28.8 us (9%)
  local copies, waits for them, and re-layouts  25.7 us (8%)
  between operations  16.8 us (5%)
  starting transfers between devices  9.44 us (3%)
  other arithmetic  7.86 us (3%)
    all_to_all x8, blocking collectives, exchange(): return lax.all_to_all(values, axes, split_axis=0, concat_axis=0, tiled=True)  160 us
    all_to_all x1, waiting for transfers between devices, exchange(): return lax.all_to_all(values, axes, split_axis=0, concat_axis=0, tiled=True)  58.9 us
    pallas_call x1, Pallas kernels, backward(): pl.pallas_call(backward_kernel, grid=(K,), in_specs=[whole(fetched.shape)...  13.6 us
    pallas_call x1, Pallas kernels, forward(): pl.pallas_call(forward_kernel, grid=(K,), in_specs=[pl.BlockSpec((targets...  11.2 us
    all_to_all x1, starting transfers between devices, exchange(): return lax.all_to_all(values, axes, split_axis=0, concat_axis=0, tiled=True)  9.4 us
    gather x1, local copies, waits for them, and re-layouts, body(): picked = jnp.take(table, asked[:, :SLOTS].reshape(-1), axis=0, mode='clip')  8.2 us
    gather x1, local copies, waits for them, and re-layouts, body(): jnp.take(got, jnp.where(late, 0, target * SLOTS + slot), axis=0, mode='cl...  7.45 us
  transfers between devices with their start and end apart: 2, of which 1 were waited for; matrix products, arithmetic and copies ran while one was open for 5% of the time, Pallas kernels for 0%

profile of v3, /device:TPU:1, one launch (start us, length us, event | category | flops | bytes accessed | tf_op | source)
XLA Modules:
  0.0 307.9 jit_solution(10787283126178596921)
XLA Ops:
  9.3 0.7 reduce.5
  10.1 3.6 %plan.1 = (bf16[64,128]{1,0:T(8,128)(2,1)S(1)}, bf16[64,128]{1,0:T(8,128)(2,1)S(1)}, s32[17,128]{1,0:T(8,128)S(1)}, s32[17,128]{1,0:T(8,128)S(1)}) custom-call(s32[17,128]{1,0:T(8,128)S(1)} %get-tuple-element.78.owner_ref, s32[17,128]{1,0:T(8,128)S(1)} %get-tuple-element.77.local_ref), custom_call_target="tpu_custom_call" | custom-call | tf_op jit(solution)/shard_map/plan/pallas_call | solution.py:136
  13.8 0.9 copy.54.scales_ref
  14.8 1.2 copy-done.2
  17.1 49.1 %all_to_all.49 = bf16[64,16,640]{2,1,0:T(8,128)(2,1)S(1)} all-to-all(bf16[64,16,640]{2,1,0:T(8,128)(2,1)S(1)} %fusion.4), channel_id=1, replica_groups=mesh['y'=8,'z'=8,'x'=4,'core'=2] {'y','z'}, dimensions={0} | all-to-all | bytes 2621440 | tf_op jit(solution)/shard_map/all_to_all | solution.py:413
  66.8 0.7 slice_reduce_fusion.1
  67.6 1.4 concatenate.22
  69.4 8.2 %gather_fusion.2 = bf16[2560,512]{1,0:T(8,128)(2,1)} fusion(bf16[2048,512]{1,0:T(8,128)(2,1)S(1)} %pad_maximum_fusion, s32[3072]{0:T(1024)S(1)} %pad_clamp_fusion.3), kind=kCustom, calls=%fused_computation.2 | custom fusion | bytes 5253120 | tf_op jit(solution)/shard_map/jit(_take)/gather | solution.py:453
  77.6 9.4 %all-to-all-start.2 = ((bf16[64,40,512]{2,1,0:T(8,128)(2,1)}), bf16[64,40,512]{2,1,0:T(8,128)(2,1)S(1)}, u32[]{:S(2)}, u32[]{:S(2)}) async-start(bf16[64,40,512]{2,1,0:T(8,128)(2,1)} %bitcast.48), calls=%async_computation.2 | async-start | bytes 5242880 | tf_op jit(solution)/shard_map/all_to_all | solution.py:413
  87.8 58.9 %all-to-all-done.2 = bf16[64,40,512]{2,1,0:T(8,128)(2,1)S(1)} async-done(((bf16[64,40,512]{2,1,0:T(8,128)(2,1)}), bf16[64,40,512]{2,1,0:T(8,128)(2,1)S(1)}, u32[]{:S(2)}, u32[]{:S(2)}) %all-to-all-start.2) | async-done | bytes 2621472 | tf_op jit(solution)/shard_map/all_to_all | solution.py:413
  146.6 7.5 %gather_fusion.3 = bf16[2112,512]{1,0:T(8,128)(2,1)} fusion(bf16[2560,512]{1,0:T(8,128)(2,1)S(1)} %bitcast.47, s32[3072]{0:T(1024)S(1)} %pad_clamp_fusion.2), kind=kCustom, calls=%fused_computation.3 | custom fusion | bytes 4333824 | tf_op jit(solution)/shard_map/jit(_take)/gather | solution.py:468
  154.1 1.4 slice_reduce_fusion
  156.4 1.7 copy-done
  158.0 1.2 copy-done.1
  159.3 11.2 %forward.1 = (bf16[1920,1024]{1,0:T(8,128)(2,1)}, bf16[192,1024]{1,0:T(8,128)(2,1)}, f32[192,1024]{1,0:T(8,128)S(1)}, f32[192,1024]{1,0:T(8,128)S(1)}, bf16[128,1152]{1,0:T(8,128)(2,1)S(1)}) custom-call(bf16[2112,512]{1,0:T(8,128)(2,1)} %get-tuple-element.79.own_ref.near_ref.fetched_ref, bf16[2112,512]{1,0:T(8,128)(2,1)} %get-tuple-element.79.own_ref.near_ref.fetched_ref, ...), custom_call_target="tpu_custom_call" | custom-call | tf_op jit(solution)/shard_map/forward/pallas_call | solution.py:257
  170.6 16.3 %all_to_all.50 = bf16[4,128,1152]{2,1,0:T(8,128)(2,1)S(1)} all-to-all(bf16[4,128,1152]{2,1,0:T(8,128)(2,1)S(1)} %broadcast_in_dim.89), channel_id=1, replica_groups=mesh['y'=8,'z'=8,'x'=4,'core'=2] {'x'}, dimensions={0} | all-to-all | bytes 2359296 | tf_op jit(solution)/shard_map/all_to_all | solution.py:413
  187.3 10.3 %all_to_all.51 = bf16[2,4,128,1152]{3,2,1,0:T(8,128)(2,1)S(1)} all-to-all(bf16[2,4,128,1152]{3,2,1,0:T(8,128)(2,1)S(1)} %broadcast_in_dim.90), channel_id=1, replica_groups=mesh['y'=8,'z'=8,'x'=4,'core'=2] {'core'}, dimensions={0} | all-to-all | bytes 4718592 | tf_op jit(solution)/shard_map/all_to_all | solution.py:413
  197.6 13.6 %backward.1 = bf16[512,1152]{1,0:T(8,128)(2,1)S(1)} custom-call(bf16[2112,512]{1,0:T(8,128)(2,1)S(1)} %copy-done.7, f32[192,10]{1,0:T(8,128)S(1)} %copy.59.importance_ref, bf16[8,1552,128]{2,1,0:T(8,128)(2,1)} %bitcast.38, bf16[1920,1024]{1,0:T(8,128)(2,1)} %get-tuple-element.43.slope_ref, bf16[192,1024]{1,0:T(8,128)(2,1)S(1)} %copy-done.3, ...), custom_call_target="tpu_custom_call" | custom-call | tf_op jit(solution)/shard_map/backward/pallas_call | solution.py:386
  211.2 4.7 %all_to_all.52 = bf16[2,256,1152]{2,1,0:T(8,128)(2,1)S(1)} all-to-all(bf16[2,256,1152]{2,1,0:T(8,128)(2,1)S(1)} %bitcast.42), channel_id=1, replica_groups=mesh['y'=8,'z'=8,'x'=4,'core'=2] {'core'}, dimensions={0} | all-to-all | bytes 2359296 | tf_op jit(solution)/shard_map/all_to_all | solution.py:413
  216.3 38.9 %all_to_all.53 = bf16[64,4,1152]{2,1,0:T(4,128)(2,1)S(1)} all-to-all(bf16[64,4,1152]{2,1,0:T(4,128)(2,1)S(1)} %reshape.167), channel_id=1, replica_groups=mesh['y'=8,'z'=8,'x'=4,'core'=2] {'y','z'}, dimensions={0} | all-to-all | bytes 1179648 | tf_op jit(solution)/shard_map/all_to_all | solution.py:413
  255.3 6.9 %all_to_all.54 = f32[4,4,1152]{2,1,0:T(4,128)S(1)} all-to-all(f32[4,4,1152]{2,1,0:T(4,128)S(1)} %broadcast_in_dim.91), channel_id=1, replica_groups=mesh['y'=8,'z'=8,'x'=4,'core'=2] {'x'}, dimensions={0} | all-to-all | bytes 147456 | tf_op jit(solution)/shard_map/all_to_all | solution.py:413
  262.4 24.6 %all_to_all.55 = bf16[64,4,1152]{2,1,0:T(4,128)(2,1)S(1)} all-to-all(bf16[64,4,1152]{2,1,0:T(4,128)(2,1)S(1)} %broadcast_in_dim.92), channel_id=1, replica_groups=mesh['y'=8,'z'=8,'x'=4,'core'=2] {'y','z'}, dimensions={0} | all-to-all | bytes 1179648 | tf_op jit(solution)/shard_map/all_to_all | solution.py:413
  287.2 9.3 %all_to_all.56 = bf16[2,256,1152]{2,1,0:T(8,128)(2,1)S(1)} all-to-all(bf16[2,256,1152]{2,1,0:T(8,128)(2,1)S(1)} %broadcast_in_dim.94), channel_id=1, replica_groups=mesh['y'=8,'z'=8,'x'=4,'core'=2] {'core'}, dimensions={0} | all-to-all | bytes 2359296 | tf_op jit(solution)/shard_map/all_to_all | solution.py:413
  297.7 1.6 slice_convert_fusion
  (60 shorter events, 7.7 us)
Async XLA Ops:
  7.2 146.9 %all-gather.3.cloned.1.call-start = ((), (), s32[]{:S(2)}) async-start(), calls=%async_computation.10 | async-start | bytes 3575808 | tf_op jit(solution)/shard_map/all_gather | solution.py:460
  14.8 1.2 copy-start.2
  69.4 8.2 %copy-start.6 = (bf16[2048,512]{1,0:T(8,128)(2,1)}, bf16[2048,512]{1,0:T(8,128)(2,1)S(1)}, u32[]{:S(2)}) copy-start(bf16[2048,512]{1,0:T(8,128)(2,1)S(1)} %pad_maximum_fusion) | copy-start | bytes 6291460
  77.6 9.8 %copy-start.8 = (f32[192,10]{0,1:T(8,128)S(1)}, f32[192,10]{0,1:T(8,128)}, u32[]{:S(2)}) copy-start(f32[192,10]{0,1:T(8,128)} %param.15) | copy-start | bytes 23044
  77.6 69.0 %all-to-all-start.2 = ((bf16[64,40,512]{2,1,0:T(8,128)(2,1)}), bf16[64,40,512]{2,1,0:T(8,128)(2,1)S(1)}, u32[]{:S(2)}, u32[]{:S(2)}) async-start(bf16[64,40,512]{2,1,0:T(8,128)(2,1)} %bitcast.48), calls=%async_computation.2 | async-start | bytes 5242880 | tf_op jit(solution)/shard_map/all_to_all | solution.py:413
  156.1 1.9 copy-start
  156.1 1.9 copy-start.4
  156.2 1.9 copy-start.5
  158.0 1.2 copy-start.1
  187.2 10.4 %copy-start.3 = (bf16[192,1024]{1,0:T(8,128)(2,1)S(1)}, bf16[192,1024]{1,0:T(8,128)(2,1)}, u32[]{:S(2)}) copy-start(bf16[192,1024]{1,0:T(8,128)(2,1)} %get-tuple-element.34.embedded_ref) | copy-start | bytes 1179652
  187.2 10.3 %copy-start.7 = (bf16[2112,512]{1,0:T(8,128)(2,1)S(1)}, bf16[2112,512]{1,0:T(8,128)(2,1)}, u32[]{:S(2)}) copy-start(bf16[2112,512]{1,0:T(8,128)(2,1)} %get-tuple-element.79.own_ref.near_ref.fetched_ref) | copy-start | bytes 6488068
Sparse Core Ops, SparseCore 0:
  69.1 32.6 all-gather.2

commit v4 on v3

--- a/solution.py
+++ b/solution.py
@@ -13,8 +13,10 @@
 ALL_SLOTS = 80
 PIECE = 16
 COPIED = 12
-TARGETS = (44, 36, 40, 40)
+TARGETS = (42, 34, 38, 36, 40, 38, 40, 40)
 DIGIT = 32
+PER = 5
+CHUNK = 256
 EXTRA = 128
 
 margin = 0.5
@@ -25,15 +27,14 @@
 GRP = ("x", "core")
 bf16 = jnp.bfloat16
 f32 = jnp.float32
-VMEM = 48 * 1024 * 1024
 
 
 def sigmoid(value):
     return 0.5 * jnp.tanh(0.5 * value) + 0.5
 
 
-def params():
-    return pltpu.CompilerParams(vmem_limit_bytes=VMEM)
+def params(megabytes=24):
+    return pltpu.CompilerParams(vmem_limit_bytes=megabytes * 1024 * 1024)
 
 
 def row_dot(a, b):
@@ -194,20 +195,25 @@
     def _():
         w_copy.start()
 
-    share = column(shares_of(importance_ref[...]), step)
-    inner = jnp.dot(near_ref[...], q_weight_ref[...], preferred_element_type=f32) + q_bias_ref[...]
-    gate = sigmoid(inner)
-    smooth = inner * gate
-    slope_ref[...] = (gate + smooth * (1.0 - gate)).astype(bf16)
-    term = share * smooth
+    targets = pooled.shape[0]
+    shares = shares_of(importance_ref[...])
+    share = [column(shares, step * PER + at) for at in range(PER)]
 
     @pl.when(step == 0)
     def _():
-        pooled[...] = term
-
-    @pl.when(step > 0)
-    def _():
-        pooled[...] += term
+        pooled[...] = jnp.zeros_like(pooled)
+
+    for part in range(pooled.shape[1] // CHUNK):
+        lanes = slice(part * CHUNK, (part + 1) * CHUNK)
+        inner = jnp.dot(near_ref[...], q_weight_ref[:, lanes], preferred_element_type=f32)
+        inner = inner + q_bias_ref[:, lanes]
+        gate = sigmoid(inner)
+        smooth = inner * gate
+        slope_ref[:, lanes] = (gate + smooth * (1.0 - gate)).astype(bf16)
+        total_term = pooled[:, lanes]
+        for at in range(PER):
+            total_term = total_term + share[at] * smooth[at * targets : (at + 1) * targets]
+        pooled[:, lanes] = total_term
 
     @pl.when(step == pl.num_programs(0) - 1)
     def _():
@@ -256,10 +262,10 @@
     sent = PAIRS + NEG_DEV
     return pl.pallas_call(
         forward_kernel,
-        grid=(K,),
+        grid=(K // PER,),
         in_specs=[
-            pl.BlockSpec((targets, width), lambda step: (0, 0)),
-            pl.BlockSpec((targets, width), lambda step: (step + 1, 0)),
+            pl.BlockSpec((targets, width), lambda step: (K, 0)),
+            pl.BlockSpec((targets * PER, width), lambda step: (step, 0)),
             whole(importance.shape),
             whole(q_weight.shape),
             whole((1, hidden)),
@@ -267,7 +273,7 @@
             whole((1, hidden)),
         ],
         out_specs=[
-            pl.BlockSpec((targets, hidden), lambda step: (step, 0)),
+            pl.BlockSpec((targets * PER, hidden), lambda step: (step, 0)),
             whole((targets, hidden)),
             whole((targets, hidden)),
             whole((targets, hidden)),
@@ -293,118 +299,112 @@
 def backward_kernel(
     fetched_ref,
     importance_ref,
-    w_ref,
-    slope_ref,
+    w_far_ref,
+    slope_far_ref,
     embedded_ref,
     active_ref,
     outer_slope_ref,
     group_ref,
     grad_ref,
-    d_pooled,
     d_inner,
-    bias_sum,
-    objective_sum,
+    w_ref,
+    w_arrived,
+    slope_ref,
+    slope_arrived,
 ):
-    step = pl.program_id(0)
+    w_copy = pltpu.make_async_copy(w_far_ref, w_ref, w_arrived)
+    slope_copy = pltpu.make_async_copy(slope_far_ref, slope_ref, slope_arrived)
+    w_copy.start()
+    slope_copy.start()
     targets, hidden = active_ref.shape
     members = group_ref.shape[0]
     negatives_count = members * NEG_DEV
 
-    @pl.when(step == 0)
-    def _():
-        embedded = embedded_ref[...]
-        queries = embedded[:PAIRS]
-        positives = embedded[PAIRS : 2 * PAIRS].astype(f32)
-        negatives = embedded[2 * PAIRS :]
-        group_queries = group_ref[:, :PAIRS, :hidden].reshape(members * PAIRS, hidden)
-        group_negatives = group_ref[:, PAIRS:, :hidden].reshape(negatives_count, hidden)
-        pieces = group_ref[:, :PAIRS, hidden:].reshape(members * PAIRS, EXTRA).astype(f32)
-        group_close = jnp.sum(pieces, axis=1, keepdims=True)
-        coef_factor = score_scale / (negatives_count * hidden)
-        wide_queries = queries.astype(f32)
-        close = jnp.sum(wide_queries * positives, axis=1, keepdims=True) / hidden
-        far = row_dot(queries, group_negatives) / hidden
-        margins = score_scale * (far - close) + margin
-        coef = (sigmoid(margins) * coef_factor).astype(bf16)
-        toward = jnp.dot(coef, group_negatives, preferred_element_type=f32)
-        row_total = jnp.sum(coef.astype(f32), axis=1, keepdims=True)
-        softplus = jnp.maximum(margins, 0.0) + jnp.log1p(jnp.exp(-jnp.abs(margins)))
-        objective = jnp.sum(jnp.sum(softplus, axis=1, keepdims=True), axis=0, keepdims=True)
-        objective_sum[...] = jnp.broadcast_to(objective / negatives_count, objective_sum.shape)
-        group_far = row_dot(group_queries, negatives) / hidden
-        group_margins = score_scale * (group_far - group_close) + margin
-        group_coef = (sigmoid(group_margins) * coef_factor).astype(bf16)
-        d_embed = jnp.concatenate(
-            [
-                toward - row_total * positives,
-                -row_total * wide_queries,
-                col_dot(group_coef, group_queries),
-            ],
-            axis=0,
-        )
-        active = active_ref[...]
-        scaling = lax.rsqrt(jnp.mean(active * active, axis=1, keepdims=True) + epsilon)
-        along = jnp.sum(d_embed * active, axis=1, keepdims=True)
-        d_active = scaling * (d_embed - active * (along * scaling * scaling / hidden))
-        d_outer = (d_active * outer_slope_ref[...]).astype(bf16)
-        width = fetched_ref.shape[1]
-        pair = 2 * w_ref.shape[2]
-        sums = jnp.zeros((targets, hidden), f32)
-        for part in range(w_ref.shape[0] // 2):
-            lanes = slice(part * pair, (part + 1) * pair)
-            sums = sums + row_dot(d_outer[:, lanes], columns(w_ref, part, width, width + hidden))
-        d_pooled[...] = sums
-        bias_sum[...] = jnp.zeros_like(bias_sum)
-
-    share = column(shares_of(importance_ref[...]), step)
-    d_near = (share * d_pooled[...] * slope_ref[...].astype(f32)).astype(bf16)
-    d_inner[pl.ds(pl.multiple_of(step * targets, targets), targets), :] = d_near
-    bias_sum[...] += jnp.sum(d_near.astype(f32), axis=0, keepdims=True)
-
-    @pl.when(step == pl.num_programs(0) - 1)
-    def _():
-        near = fetched_ref[targets:, :]
-        for part in range(4):
-            lanes = slice(part * hidden // 4, (part + 1) * hidden // 4)
-            grad_ref[:, lanes] = col_dot(near, d_inner[:, lanes]).astype(bf16)
-        grad_ref[:, hidden:] = jnp.zeros((grad_ref.shape[0], EXTRA), bf16)
-        rows = lax.broadcasted_iota(jnp.int32, (16, EXTRA), 0)
-        small = jnp.zeros((16, EXTRA), f32)
-        for part in range(hidden // EXTRA):
-            piece = bias_sum[:, part * EXTRA : (part + 1) * EXTRA]
-            small = jnp.where(rows == part, piece, small)
-        objective = objective_sum[...]
-        first = objective.astype(bf16).astype(f32)
-        small = jnp.where(rows == hidden // EXTRA, first, small)
-        small = jnp.where(rows == hidden // EXTRA + 1, objective - first, small)
-        grad_ref[:16, hidden:] = small.astype(bf16)
+    embedded = embedded_ref[...]
+    queries = embedded[:PAIRS]
+    positives = embedded[PAIRS : 2 * PAIRS].astype(f32)
+    negatives = embedded[2 * PAIRS :]
+    group_queries = group_ref[:, :PAIRS, :hidden].reshape(members * PAIRS, hidden)
+    group_negatives = group_ref[:, PAIRS:, :hidden].reshape(negatives_count, hidden)
+    pieces = group_ref[:, :PAIRS, hidden:].reshape(members * PAIRS, EXTRA).astype(f32)
+    group_close = jnp.sum(pieces, axis=1, keepdims=True)
+    coef_factor = score_scale / (negatives_count * hidden)
+    wide_queries = queries.astype(f32)
+    close = jnp.sum(wide_queries * positives, axis=1, keepdims=True) / hidden
+    far = row_dot(queries, group_negatives) / hidden
+    margins = score_scale * (far - close) + margin
+    coef = (sigmoid(margins) * coef_factor).astype(bf16)
+    toward = jnp.dot(coef, group_negatives, preferred_element_type=f32)
+    row_total = jnp.sum(coef.astype(f32), axis=1, keepdims=True)
+    softplus = jnp.maximum(margins, 0.0) + jnp.log1p(jnp.exp(-jnp.abs(margins)))
+    objective = jnp.sum(jnp.sum(softplus, axis=1, keepdims=True), axis=0, keepdims=True)
+    objective = objective / negatives_count
+    group_far = row_dot(group_queries, negatives) / hidden
+    group_margins = score_scale * (group_far - group_close) + margin
+    group_coef = (sigmoid(group_margins) * coef_factor).astype(bf16)
+    d_embed = jnp.concatenate(
+        [
+            toward - row_total * positives,
+            -row_total * wide_queries,
+            col_dot(group_coef, group_queries),
+        ],
+        axis=0,
+    )
+    active = active_ref[...]
+    scaling = lax.rsqrt(jnp.mean(active * active, axis=1, keepdims=True) + epsilon)
+    along = jnp.sum(d_embed * active, axis=1, keepdims=True)
+    d_active = scaling * (d_embed - active * (along * scaling * scaling / hidden))
+    d_outer = (d_active * outer_slope_ref[...]).astype(bf16)
+    w_copy.wait()
+    width = fetched_ref.shape[1]
+    pair = 2 * w_ref.shape[2]
+    sums = jnp.zeros((targets, hidden), f32)
+    for part in range(w_ref.shape[0] // 2):
+        lanes = slice(part * pair, (part + 1) * pair)
+        sums = sums + row_dot(d_outer[:, lanes], columns(w_ref, part, width, width + hidden))
+    d_pooled = sums
+
+    shares = shares_of(importance_ref[...])
+    sums = jnp.zeros((1, hidden), f32)
+    slope_copy.wait()
+    for at in range(K):
+        rows = slice(at * targets, (at + 1) * targets)
+        d_near = (column(shares, at) * d_pooled * slope_ref[rows, :].astype(f32)).astype(bf16)
+        d_inner[rows, :] = d_near
+        sums = sums + jnp.sum(d_near.astype(f32), axis=0, keepdims=True)
+
+    near = fetched_ref[: K * targets, :]
+    grad_ref[:, :hidden] = col_dot(near, d_inner[...]).astype(bf16)
+    grad_ref[:, hidden:] = jnp.zeros((grad_ref.shape[0], EXTRA), bf16)
+    rows = lax.broadcasted_iota(jnp.int32, (16, EXTRA), 0)
+    small = jnp.zeros((16, EXTRA), f32)
+    for part in range(hidden // EXTRA):
+        piece = sums[:, part * EXTRA : (part + 1) * EXTRA]
+        small = jnp.where(rows == part, piece, small)
+    first = objective.astype(bf16).astype(f32)
+    small = jnp.where(rows == hidden // EXTRA, first, small)
+    small = jnp.where(rows == hidden // EXTRA + 1, objective - first, small)
+    grad_ref[:16, hidden:] = small.astype(bf16)
 
 
 def backward(fetched, importance, w_full, slope, embedded, active, outer_slope, group):
     targets, hidden = active.shape
     width = fetched.shape[1]
+    far = pl.BlockSpec(memory_space=pl.ANY)
+    near = pl.BlockSpec(memory_space=pltpu.VMEM)
     return pl.pallas_call(
         backward_kernel,
-        grid=(K,),
-        in_specs=[
-            whole(fetched.shape),
-            whole(importance.shape),
-            whole(w_full.shape),
-            pl.BlockSpec((targets, hidden), lambda step: (step, 0)),
-            whole(embedded.shape),
-            whole(active.shape),
-            whole(outer_slope.shape),
-            whole(group.shape),
-        ],
-        out_specs=whole((width, hidden + EXTRA)),
+        in_specs=[near, near, far, far, near, near, near, near],
+        out_specs=near,
         out_shape=jax.ShapeDtypeStruct((width, hidden + EXTRA), bf16),
         scratch_shapes=[
-            pltpu.VMEM((targets, hidden), f32),
             pltpu.VMEM((targets * K, hidden), bf16),
-            pltpu.VMEM((1, hidden), f32),
-            pltpu.VMEM((1, EXTRA), f32),
+            pltpu.VMEM(w_full.shape, bf16),
+            pltpu.SemaphoreType.DMA,
+            pltpu.VMEM(slope.shape, bf16),
+            pltpu.SemaphoreType.DMA,
         ],
-        compiler_params=params(),
+        compiler_params=params(36),
         name="backward",
     )(fetched, importance, w_full, slope, embedded, active, outer_slope, group)
 
@@ -458,10 +458,10 @@
     over = jnp.max(sent[:, COPIED + 2, 127])
     w_part = jnp.concatenate([w_part, jnp.broadcast_to(over, (16, lanes))], axis=0)
     w_full = lax.all_gather(w_part, GRP, axis=0, tiled=False)
-    over = jnp.max(w_full[:, -16:, :].astype(f32)) > 0.5
+    over = jnp.max(w_full[:, -1, :1].astype(f32)) > 0.5
 
     def ordered(values):
-        return values.reshape(targets, K + 1).T.reshape(-1)
+        return jnp.roll(values.reshape(targets, K + 1).T, -1, axis=0).reshape(-1)
 
     target, slot = ordered(target), ordered(slot)
     late = slot >= SLOTS

time: 309 us -> 301 us (0.974)
  Pallas kernels: 28.8 us -> 20.9 us
    pallas_call x2, Pallas kernels: 24.8 us -> 14.9 us  [the longest x1 8.28 us: forward(): pl.pallas_call(forward_kernel, grid=(K // PER,), in_specs=[pl.BlockSpec((...]
  transfers between devices with their start and end apart: 2 -> 2, of which waited for: 1 -> 1; matrix products, arithmetic and copies ran while one was open for 5% -> 6% of each run, Pallas kernels for 0% -> 0%
where the time goes in v4:
time: 301 us; the launch traced here: 300 us
  blocking collectives  160 us (53%)
  waiting for transfers between devices  58.4 us (19%)
  local copies, waits for them, and re-layouts  26.1 us (9%)
  Pallas kernels  20.9 us (7%)
  between operations  16.8 us (6%)
  starting transfers between devices  9.44 us (3%)
  other arithmetic  7.82 us (3%)
    all_to_all x8, blocking collectives, exchange(): return lax.all_to_all(values, axes, split_axis=0, concat_axis=0, tiled=True)  160 us
    all_to_all x1, waiting for transfers between devices, exchange(): return lax.all_to_all(values, axes, split_axis=0, concat_axis=0, tiled=True)  58.4 us
    all_to_all x1, starting transfers between devices, exchange(): return lax.all_to_all(values, axes, split_axis=0, concat_axis=0, tiled=True)  9.4 us
    pallas_call x1, Pallas kernels, forward(): pl.pallas_call(forward_kernel, grid=(K // PER,), in_specs=[pl.BlockSpec((...  8.28 us
    gather x1, local copies, waits for them, and re-layouts, body(): picked = jnp.take(table, asked[:, :SLOTS].reshape(-1), axis=0, mode='clip')  8.21 us
    gather x1, local copies, waits for them, and re-layouts, body(): jnp.take(got, jnp.where(late, 0, target * SLOTS + slot), axis=0, mode='cl...  7.45 us
    pallas_call x1, Pallas kernels, backward(): pl.pallas_call(backward_kernel, in_specs=[near, near, far, far, near, nea...  6.6 us
  transfers between devices with their start and end apart: 2, of which 1 were waited for; matrix products, arithmetic and copies ran while one was open for 6% of the time, Pallas kernels for 0%

profile of v4, /device:TPU:1, one launch (start us, length us, event | category | flops | bytes accessed | tf_op | source)
XLA Modules:
  0.0 300.0 jit_solution(3859401144509635422)
XLA Ops:
  9.3 0.7 reduce.7
  10.1 5.7 %plan.1 = (bf16[64,128]{1,0:T(8,128)(2,1)S(1)}, bf16[64,128]{1,0:T(8,128)(2,1)S(1)}, s32[17,128]{1,0:T(8,128)S(1)}, s32[17,128]{1,0:T(8,128)S(1)}) custom-call(s32[17,128]{1,0:T(8,128)S(1)} %get-tuple-element.61.owner_ref, s32[17,128]{1,0:T(8,128)S(1)} %get-tuple-element.60.local_ref), custom_call_target="tpu_custom_call" | custom-call | tf_op jit(solution)/shard_map/plan/pallas_call | solution.py:137
  15.9 0.9 copy.65.scales_ref
  16.8 1.2 copy-done.2
  19.1 49.1 %all_to_all.49 = bf16[64,16,640]{2,1,0:T(8,128)(2,1)S(1)} all-to-all(bf16[64,16,640]{2,1,0:T(8,128)(2,1)S(1)} %fusion.4), channel_id=1, replica_groups=mesh['y'=8,'z'=8,'x'=4,'core'=2] {'y','z'}, dimensions={0} | all-to-all | bytes 2621440 | tf_op jit(solution)/shard_map/all_to_all | solution.py:413
  68.9 0.7 slice_reduce_fusion
  69.6 1.4 concatenate.29
  71.5 8.2 %gather_fusion.2 = bf16[2560,512]{1,0:T(8,128)(2,1)} fusion(bf16[2048,512]{1,0:T(8,128)(2,1)S(1)} %pad_maximum_fusion, s32[3072]{0:T(1024)S(1)} %pad_clamp_fusion.3), kind=kCustom, calls=%fused_computation.2 | custom fusion | bytes 5253120 | tf_op jit(solution)/shard_map/jit(_take)/gather | solution.py:453
  79.7 9.4 %all-to-all-start.2 = ((bf16[64,40,512]{2,1,0:T(8,128)(2,1)}), bf16[64,40,512]{2,1,0:T(8,128)(2,1)S(1)}, u32[]{:S(2)}, u32[]{:S(2)}) async-start(bf16[64,40,512]{2,1,0:T(8,128)(2,1)} %bitcast.48), calls=%async_computation.2 | async-start | bytes 5242880 | tf_op jit(solution)/shard_map/all_to_all | solution.py:413
  90.3 58.4 %all-to-all-done.2 = bf16[64,40,512]{2,1,0:T(8,128)(2,1)S(1)} async-done(((bf16[64,40,512]{2,1,0:T(8,128)(2,1)}), bf16[64,40,512]{2,1,0:T(8,128)(2,1)S(1)}, u32[]{:S(2)}, u32[]{:S(2)}) %all-to-all-start.2) | async-done | bytes 2621472 | tf_op jit(solution)/shard_map/all_to_all | solution.py:413
  148.7 7.4 %gather_fusion.3 = bf16[2112,512]{1,0:T(8,128)(2,1)} fusion(bf16[2560,512]{1,0:T(8,128)(2,1)S(1)} %bitcast.47, s32[3072]{0:T(1024)S(1)} %pad_clamp_fusion.2), kind=kCustom, calls=%fused_computation.3 | custom fusion | bytes 4333824 | tf_op jit(solution)/shard_map/jit(_take)/gather | solution.py:468
  156.1 1.3 slice_reduce_fusion.1
  158.4 1.6 copy-done
  160.0 1.2 copy-done.1
  161.3 8.3 %forward.1 = (bf16[1920,1024]{1,0:T(8,128)(2,1)S(1)}, bf16[192,1024]{1,0:T(8,128)(2,1)}, f32[192,1024]{1,0:T(8,128)S(1)}, f32[192,1024]{1,0:T(8,128)S(1)}, bf16[128,1152]{1,0:T(8,128)(2,1)S(1)}) custom-call(bf16[2112,512]{1,0:T(8,128)(2,1)} %get-tuple-element.62.own_ref.near_ref.fetched_ref, ...), custom_call_target="tpu_custom_call" | custom-call | tf_op jit(solution)/shard_map/forward/pallas_call | solution.py:263
  169.6 16.3 %all_to_all.50 = bf16[4,128,1152]{2,1,0:T(8,128)(2,1)S(1)} all-to-all(bf16[4,128,1152]{2,1,0:T(8,128)(2,1)S(1)} %broadcast_in_dim.89), channel_id=1, replica_groups=mesh['y'=8,'z'=8,'x'=4,'core'=2] {'x'}, dimensions={0} | all-to-all | bytes 2359296 | tf_op jit(solution)/shard_map/all_to_all | solution.py:413
  186.3 10.3 %all_to_all.51 = bf16[2,4,128,1152]{3,2,1,0:T(8,128)(2,1)S(1)} all-to-all(bf16[2,4,128,1152]{3,2,1,0:T(8,128)(2,1)S(1)} %broadcast_in_dim.90), channel_id=1, replica_groups=mesh['y'=8,'z'=8,'x'=4,'core'=2] {'core'}, dimensions={0} | all-to-all | bytes 4718592 | tf_op jit(solution)/shard_map/all_to_all | solution.py:413
  196.6 6.6 %backward.1 = bf16[512,1152]{1,0:T(8,128)(2,1)S(1)} custom-call(bf16[2112,512]{1,0:T(8,128)(2,1)S(1)} %copy-done.7, f32[192,10]{1,0:T(8,128)S(1)} %copy.71.importance_ref, bf16[8,1552,128]{2,1,0:T(8,128)(2,1)S(1)} %bitcast.39, bf16[1920,1024]{1,0:T(8,128)(2,1)S(1)} %get-tuple-element.43.slope_far_ref, bf16[192,1024]{1,0:T(8,128)(2,1)S(1)} %copy-done.3, ...), custom_call_target="tpu_custom_call" | custom-call | tf_op jit(solution)/shard_map/backward/pallas_call | solution.py:395
  203.2 4.7 %all_to_all.52 = bf16[2,256,1152]{2,1,0:T(8,128)(2,1)S(1)} all-to-all(bf16[2,256,1152]{2,1,0:T(8,128)(2,1)S(1)} %bitcast.42), channel_id=1, replica_groups=mesh['y'=8,'z'=8,'x'=4,'core'=2] {'core'}, dimensions={0} | all-to-all | bytes 2359296 | tf_op jit(solution)/shard_map/all_to_all | solution.py:413
  208.3 39.0 %all_to_all.53 = bf16[64,4,1152]{2,1,0:T(4,128)(2,1)S(1)} all-to-all(bf16[64,4,1152]{2,1,0:T(4,128)(2,1)S(1)} %reshape.168), channel_id=1, replica_groups=mesh['y'=8,'z'=8,'x'=4,'core'=2] {'y','z'}, dimensions={0} | all-to-all | bytes 1179648 | tf_op jit(solution)/shard_map/all_to_all | solution.py:413
  247.4 6.9 %all_to_all.54 = f32[4,4,1152]{2,1,0:T(4,128)S(1)} all-to-all(f32[4,4,1152]{2,1,0:T(4,128)S(1)} %broadcast_in_dim.91), channel_id=1, replica_groups=mesh['y'=8,'z'=8,'x'=4,'core'=2] {'x'}, dimensions={0} | all-to-all | bytes 147456 | tf_op jit(solution)/shard_map/all_to_all | solution.py:413
  254.5 24.6 %all_to_all.55 = bf16[64,4,1152]{2,1,0:T(4,128)(2,1)S(1)} all-to-all(bf16[64,4,1152]{2,1,0:T(4,128)(2,1)S(1)} %broadcast_in_dim.92), channel_id=1, replica_groups=mesh['y'=8,'z'=8,'x'=4,'core'=2] {'y','z'}, dimensions={0} | all-to-all | bytes 1179648 | tf_op jit(solution)/shard_map/all_to_all | solution.py:413
  279.2 9.3 %all_to_all.56 = bf16[2,256,1152]{2,1,0:T(8,128)(2,1)S(1)} all-to-all(bf16[2,256,1152]{2,1,0:T(8,128)(2,1)S(1)} %broadcast_in_dim.94), channel_id=1, replica_groups=mesh['y'=8,'z'=8,'x'=4,'core'=2] {'core'}, dimensions={0} | all-to-all | bytes 2359296 | tf_op jit(solution)/shard_map/all_to_all | solution.py:413
  289.8 1.6 slice_convert_fusion
  (65 shorter events, 8.2 us)
Async XLA Ops:
  7.2 149.0 %all-gather.3.cloned.1.call-start = ((), (), s32[]{:S(2)}) async-start(), calls=%async_computation.10 | async-start | bytes 3575808 | tf_op jit(solution)/shard_map/all_gather | solution.py:460
  16.8 1.2 copy-start.2
  71.5 8.2 %copy-start.6 = (bf16[2048,512]{1,0:T(8,128)(2,1)}, bf16[2048,512]{1,0:T(8,128)(2,1)S(1)}, u32[]{:S(2)}) copy-start(bf16[2048,512]{1,0:T(8,128)(2,1)S(1)} %pad_maximum_fusion) | copy-start | bytes 6291460
  79.7 9.4 %copy-start.8 = (f32[192,10]{0,1:T(8,128)S(1)}, f32[192,10]{0,1:T(8,128)}, u32[]{:S(2)}) copy-start(f32[192,10]{0,1:T(8,128)} %param.15) | copy-start | bytes 23044
  79.7 69.0 %all-to-all-start.2 = ((bf16[64,40,512]{2,1,0:T(8,128)(2,1)}), bf16[64,40,512]{2,1,0:T(8,128)(2,1)S(1)}, u32[]{:S(2)}, u32[]{:S(2)}) async-start(bf16[64,40,512]{2,1,0:T(8,128)(2,1)} %bitcast.48), calls=%async_computation.2 | async-start | bytes 5242880 | tf_op jit(solution)/shard_map/all_to_all | solution.py:413
  158.1 1.9 copy-start
  158.1 1.9 copy-start.4
  158.2 1.9 copy-start.5
  160.0 1.2 copy-start.1
  186.3 10.4 %copy-start.3 = (bf16[192,1024]{1,0:T(8,128)(2,1)S(1)}, bf16[192,1024]{1,0:T(8,128)(2,1)}, u32[]{:S(2)}) copy-start(bf16[192,1024]{1,0:T(8,128)(2,1)} %get-tuple-element.34.embedded_ref) | copy-start | bytes 1179652
  186.3 10.4 %copy-start.7 = (bf16[2112,512]{1,0:T(8,128)(2,1)S(1)}, bf16[2112,512]{1,0:T(8,128)(2,1)}, u32[]{:S(2)}) copy-start(bf16[2112,512]{1,0:T(8,128)(2,1)} %get-tuple-element.62.own_ref.near_ref.fetched_ref) | copy-start | bytes 6488068
Sparse Core Ops, SparseCore 0:
  71.2 32.6 all-gather.2

commit v5 on v4

--- a/solution.py
+++ b/solution.py
@@ -67,12 +67,26 @@
     return jnp.sum(wide * values, axis=0, keepdims=True)
 
 
-def plan_kernel(owner_ref, local_ref, high_ref, low_ref, target_ref, slot_ref):
-    blocks, width = owner_ref.shape
-    owners = high_ref.shape[0]
+def plan_kernel(
+    row_ref,
+    slab_far_ref,
+    scales_ref,
+    w_ref,
+    sent_ref,
+    ready_ref,
+    target_ref,
+    slot_ref,
+    slab_ref,
+    slab_arrived,
+):
+    slab_copy = pltpu.make_async_copy(slab_far_ref, slab_ref, slab_arrived)
+    slab_copy.start()
+    blocks, width = row_ref.shape
+    pins = ready_ref.shape[0]
+    owners = pins // PIECE
     ids = lax.broadcasted_iota(jnp.int32, (owners, width), 0)
-    own = [owner_ref[block : block + 1, :] for block in range(blocks)]
-    local = [local_ref[block : block + 1, :] for block in range(blocks)]
+    own = [row_ref[block : block + 1, :] // pins for block in range(blocks)]
+    local = [row_ref[block : block + 1, :] % pins for block in range(blocks)]
     first = [(one == ids).astype(f32) for one in own]
     second = [((one // PIECE) == ids).astype(f32) for one in local]
     free = [jnp.where(one % PIECE < COPIED, 1.0, 0.0) for one in local]
@@ -124,36 +138,55 @@
         slot_ref[block : block + 1, :] = slot
     late = (jnp.max(widest, axis=1, keepdims=True) >= SLOTS).astype(f32)
     last = lax.broadcasted_iota(jnp.int32, (owners, width), 1) == width - 1
-    high_ref[...] = jnp.where(last, late, high_sum).astype(bf16)
-    low_ref[...] = low_sum.astype(bf16)
-
-
-def plan(owner, local, owners):
-    rows = owner.shape[0]
-    blocks = -(-rows // 128)
-    spare = blocks * 128 - rows
-    owner = jnp.pad(owner[:, 0], (0, spare), constant_values=owners).reshape(blocks, 128)
-    local = jnp.pad(local[:, 0], (0, spare)).reshape(blocks, 128)
-    high, low, target, slot = pl.pallas_call(
-        plan_kernel,
-        out_shape=(
-            jax.ShapeDtypeStruct((owners, 128), bf16),
-            jax.ShapeDtypeStruct((owners, 128), bf16),
-            jax.ShapeDtypeStruct((blocks, 128), jnp.int32),
-            jax.ShapeDtypeStruct((blocks, 128), jnp.int32),
-        ),
-        compiler_params=params(),
-        name="plan",
-    )(owner, local)
-    return high, low, target.reshape(-1)[:rows], slot.reshape(-1)[:rows]
-
-
-def dequantize_kernel(slab_ref, scales_ref, out_ref):
+    digits = jnp.concatenate([jnp.where(last, late, high_sum), low_sum], axis=1).astype(bf16)
+    slab_copy.wait()
     block = slab_ref.shape[1] // scales_ref.shape[1]
     for part in range(scales_ref.shape[1]):
         lanes = slice(part * block, (part + 1) * block)
         scale = scales_ref[:, part : part + 1].astype(f32)
-        out_ref[:, lanes] = (slab_ref[:, lanes].astype(f32) * scale).astype(bf16)
+        ready_ref[:, lanes] = (slab_ref[:, lanes].astype(f32) * scale).astype(bf16)
+    here = COPIED + 2
+    piece_row = lax.broadcasted_iota(jnp.int32, (pins, owners), 1) * PIECE + here
+    rows = lax.broadcasted_iota(jnp.int32, (pins, owners), 0)
+    digits = jnp.dot(
+        (rows == piece_row).astype(f32).astype(bf16), digits, preferred_element_type=f32
+    )
+    place = lax.broadcasted_iota(jnp.int32, (pins, block), 0) % PIECE
+    w_part = w_ref[...].astype(f32)
+    for part in range(scales_ref.shape[1]):
+        lanes = slice(part * block, (part + 1) * block)
+        values = ready_ref[:, lanes].astype(f32)
+        values = jnp.where(place == COPIED, w_part[PIECE + part : PIECE + part + 1], values)
+        values = jnp.where(place == COPIED + 1, w_part[PIECE + 4 + part : PIECE + 5 + part], values)
+        if part < 2:
+            values = jnp.where(place == here, digits[:, lanes], values)
+        sent_ref[:, lanes] = values.astype(bf16)
+    side = jnp.broadcast_to(w_part[None, :PIECE], (owners, PIECE, block)).reshape(pins, block)
+    sent_ref[:, scales_ref.shape[1] * block :] = side.astype(bf16)
+
+
+def plan(slab, scales, w_part, owner, local, owners):
+    rows = owner.shape[0]
+    pins = slab.shape[0]
+    blocks = -(-rows // 128)
+    spare = blocks * 128 - rows
+    row = (owner * pins + local)[:, 0]
+    row = jnp.pad(row, (0, spare), constant_values=owners * pins).reshape(blocks, 128)
+    near = pl.BlockSpec(memory_space=pltpu.VMEM)
+    sent, ready, target, slot = pl.pallas_call(
+        plan_kernel,
+        in_specs=[near, pl.BlockSpec(memory_space=pl.ANY), near, near],
+        out_shape=(
+            jax.ShapeDtypeStruct((pins, slab.shape[1] + w_part.shape[1]), bf16),
+            jax.ShapeDtypeStruct(slab.shape, bf16),
+            jax.ShapeDtypeStruct((blocks, 128), jnp.int32),
+            jax.ShapeDtypeStruct((blocks, 128), jnp.int32),
+        ),
+        scratch_shapes=[pltpu.VMEM(slab.shape, bf16), pltpu.SemaphoreType.DMA],
+        compiler_params=params(),
+        name="plan",
+    )(row, slab, scales, w_part)
+    return sent, ready, target.reshape(-1)[:rows], slot.reshape(-1)[:rows]
 
 
 def shares_of(importance):
@@ -429,26 +462,15 @@
     pin_count = lax.axis_size(PIN)
     targets = importance.shape[0]
     width, hidden = q_weight.shape
-    high, low, target, slot = plan(owner, local, pin_count)
-    ready = pl.pallas_call(
-        dequantize_kernel,
-        out_shape=jax.ShapeDtypeStruct(slab.shape, bf16),
-        compiler_params=params(),
-        name="dequantize",
-    )(slab, scales)
-    members = lax.axis_size(GRP)
-    lanes = hidden // members
+    lanes = hidden // lax.axis_size(GRP)
     rows = w_weight.shape[0]
-    mine = lax.dynamic_slice_in_dim(w_weight, lax.axis_index(GRP) * lanes, lanes, 1)
-    tail = jnp.broadcast_to(mine[PIECE:].reshape(1, 2, width), (pin_count, 2, width))
-    ids = jnp.pad(jnp.concatenate([high, low], axis=1), ((0, 0), (0, width - 256)))
-    tail = jnp.concatenate([tail, jnp.pad(ids[:, None], ((0, 0), (0, 1), (0, 0)))], axis=1)
-    sent = jnp.concatenate([ready.reshape(pin_count, PIECE, width)[:, :COPIED], tail], axis=1)
-    side = jnp.broadcast_to(mine[None, :PIECE], (pin_count, PIECE, lanes))
-    sent = exchange(jnp.concatenate([sent, side], axis=2), PIN)
+    w_part = lax.dynamic_slice_in_dim(w_weight, lax.axis_index(GRP) * lanes, lanes, 1)
+    sent, ready, target, slot = plan(slab, scales, w_part, owner, local, pin_count)
+    sent = exchange(sent.reshape(pin_count, PIECE, width + lanes), PIN)
     table = sent[:, :, :width].reshape(pin_count * PIECE, width)
     table = jnp.concatenate([ready, table], axis=0)
-    ids = sent[:, COPIED + 2].astype(jnp.int32)
+    digits = sent[:, COPIED + 2, :256]
+    ids = digits.astype(jnp.int32)
     asked = ids[:, :ALL_SLOTS] * DIGIT + ids[:, 128 : 128 + ALL_SLOTS]
     picked = jnp.take(table, asked[:, :SLOTS].reshape(-1), axis=0, mode="clip")
     got = exchange(picked.reshape(pin_count, SLOTS, width), PIN).reshape(-1, width)

time: 301 us -> 298 us (0.990)
    pallas_call x2 -> x1, Pallas kernels: 6.06 us -> 6.64 us  [plan(): pl.pallas_call(plan_kernel, in_specs=[near, pl.BlockSpec(memory_space=pl....]
where the time goes in v5:
time: 298 us; the launch traced here: 297 us
  blocking collectives  160 us (54%)
  waiting for transfers between devices  58.4 us (20%)
  local copies, waits for them, and re-layouts  24.6 us (8%)
  Pallas kernels  21.5 us (7%)
  between operations  16.8 us (6%)
  starting transfers between devices  9.44 us (3%)
  other arithmetic  6.3 us (2%)
    all_to_all x8, blocking collectives, exchange(): return lax.all_to_all(values, axes, split_axis=0, concat_axis=0, tiled=True)  160 us
    all_to_all x1, waiting for transfers between devices, exchange(): return lax.all_to_all(values, axes, split_axis=0, concat_axis=0, tiled=True)  58.4 us
    all_to_all x1, starting transfers between devices, exchange(): return lax.all_to_all(values, axes, split_axis=0, concat_axis=0, tiled=True)  9.4 us
    pallas_call x1, Pallas kernels, forward(): pl.pallas_call(forward_kernel, grid=(K // PER,), in_specs=[pl.BlockSpec((...  8.26 us
    gather x1, local copies, waits for them, and re-layouts, body(): picked = jnp.take(table, asked[:, :SLOTS].reshape(-1), axis=0, mode='clip')  8.22 us
    gather x1, local copies, waits for them, and re-layouts, body(): jnp.take(got, jnp.where(late, 0, target * SLOTS + slot), axis=0, mode='cl...  7.44 us
    pallas_call x1, Pallas kernels, plan(): pl.pallas_call(plan_kernel, in_specs=[near, pl.BlockSpec(memory_space=pl....  6.64 us
    pallas_call x1, Pallas kernels, backward(): pl.pallas_call(backward_kernel, in_specs=[near, near, far, far, near, nea...  6.6 us
  transfers between devices with their start and end apart: 2, of which 1 were waited for; matrix products, arithmetic and copies ran while one was open for 6% of the time, Pallas kernels for 0%

profile of v5, /device:TPU:1, one launch (start us, length us, event | category | flops | bytes accessed | tf_op | source)
XLA Modules:
  0.0 297.2 jit_solution(8254902582807440409)
XLA Ops:
  7.2 0.7 add_reduce_fusion
  8.0 0.9 copy.59.scales_ref
  8.9 1.2 copy-done.3
  10.2 6.6 %plan.1 = (bf16[1024,640]{1,0:T(8,128)(2,1)S(1)}, bf16[1024,512]{1,0:T(8,128)(2,1)S(1)}, s32[17,128]{1,0:T(8,128)S(1)}, s32[17,128]{1,0:T(8,128)S(1)}) custom-call(s32[17,128]{1,0:T(8,128)S(1)} %pad_bitcast_fusion.row_ref, bf16[1024,512]{1,0:T(8,128)(2,1)S(1)} %copy-done.3, bf16[1024,4]{1,0:T(8,128)(2,1)S(1)} %copy.59.scales_ref, ...), custom_call_target="tpu_custom_call" | custom-call | tf_op jit(solution)/shard_map/plan/pallas_call | solution.py:176
  16.8 49.1 %all_to_all.49 = bf16[64,16,640]{2,1,0:T(8,128)(2,1)S(1)} all-to-all(bf16[64,16,640]{2,1,0:T(8,128)(2,1)S(1)} %bitcast.37), channel_id=1, replica_groups=mesh['y'=8,'z'=8,'x'=4,'core'=2] {'y','z'}, dimensions={0} | all-to-all | bytes 2621440 | tf_op jit(solution)/shard_map/all_to_all | solution.py:446
  66.4 0.7 slice_reduce_fusion
  67.1 1.4 concatenate.17
  69.0 8.2 %gather_fusion.2 = bf16[2560,512]{1,0:T(8,128)(2,1)} fusion(bf16[2048,512]{1,0:T(8,128)(2,1)S(1)} %pad_maximum_fusion, s32[3072]{0:T(1024)S(1)} %pad_clamp_fusion.3), kind=kCustom, calls=%fused_computation.2 | custom fusion | bytes 5253120 | tf_op jit(solution)/shard_map/jit(_take)/gather | solution.py:475
  77.2 9.4 %all-to-all-start.2 = ((bf16[64,40,512]{2,1,0:T(8,128)(2,1)}), bf16[64,40,512]{2,1,0:T(8,128)(2,1)S(1)}, u32[]{:S(2)}, u32[]{:S(2)}) async-start(bf16[64,40,512]{2,1,0:T(8,128)(2,1)} %bitcast.43), calls=%async_computation.2 | async-start | bytes 5242880 | tf_op jit(solution)/shard_map/all_to_all | solution.py:446
  87.8 58.4 %all-to-all-done.2 = bf16[64,40,512]{2,1,0:T(8,128)(2,1)S(1)} async-done(((bf16[64,40,512]{2,1,0:T(8,128)(2,1)}), bf16[64,40,512]{2,1,0:T(8,128)(2,1)S(1)}, u32[]{:S(2)}, u32[]{:S(2)}) %all-to-all-start.2) | async-done | bytes 2621472 | tf_op jit(solution)/shard_map/all_to_all | solution.py:446
  146.2 7.4 %gather_fusion.3 = bf16[2112,512]{1,0:T(8,128)(2,1)} fusion(bf16[2560,512]{1,0:T(8,128)(2,1)S(1)} %bitcast.42, s32[3072]{0:T(1024)S(1)} %pad_clamp_fusion.2), kind=kCustom, calls=%fused_computation.3 | custom fusion | bytes 4333824 | tf_op jit(solution)/shard_map/jit(_take)/gather | solution.py:490
  153.7 1.3 slice_reduce_fusion.1
  155.9 1.6 copy-done.1
  157.6 1.2 copy-done.2
  158.8 8.3 %forward.1 = (bf16[1920,1024]{1,0:T(8,128)(2,1)S(1)}, bf16[192,1024]{1,0:T(8,128)(2,1)}, f32[192,1024]{1,0:T(8,128)S(1)}, f32[192,1024]{1,0:T(8,128)S(1)}, bf16[128,1152]{1,0:T(8,128)(2,1)S(1)}) custom-call(bf16[2112,512]{1,0:T(8,128)(2,1)} %get-tuple-element.60.own_ref.near_ref.fetched_ref, ...), custom_call_target="tpu_custom_call" | custom-call | tf_op jit(solution)/shard_map/forward/pallas_call | solution.py:296
  167.2 16.6 %all_to_all.50 = bf16[4,128,1152]{2,1,0:T(8,128)(2,1)S(1)} all-to-all(bf16[4,128,1152]{2,1,0:T(8,128)(2,1)S(1)} %broadcast_in_dim.69), channel_id=1, replica_groups=mesh['y'=8,'z'=8,'x'=4,'core'=2] {'x'}, dimensions={0} | all-to-all | bytes 2359296 | tf_op jit(solution)/shard_map/all_to_all | solution.py:446
  184.1 10.1 %all_to_all.51 = bf16[2,4,128,1152]{3,2,1,0:T(8,128)(2,1)S(1)} all-to-all(bf16[2,4,128,1152]{3,2,1,0:T(8,128)(2,1)S(1)} %broadcast_in_dim.70), channel_id=1, replica_groups=mesh['y'=8,'z'=8,'x'=4,'core'=2] {'core'}, dimensions={0} | all-to-all | bytes 4718592 | tf_op jit(solution)/shard_map/all_to_all | solution.py:446
  194.2 6.6 %backward.1 = bf16[512,1152]{1,0:T(8,128)(2,1)S(1)} custom-call(bf16[2112,512]{1,0:T(8,128)(2,1)S(1)} %copy-done.8, f32[192,10]{1,0:T(8,128)S(1)} %copy.64.importance_ref, bf16[8,1552,128]{2,1,0:T(8,128)(2,1)S(1)} %bitcast.34, bf16[1920,1024]{1,0:T(8,128)(2,1)S(1)} %get-tuple-element.43.slope_far_ref, bf16[192,1024]{1,0:T(8,128)(2,1)S(1)} %copy-done.4, ...), custom_call_target="tpu_custom_call" | custom-call | tf_op jit(solution)/shard_map/backward/pallas_call | solution.py:428
  200.8 4.7 %all_to_all.52 = bf16[2,256,1152]{2,1,0:T(8,128)(2,1)S(1)} all-to-all(bf16[2,256,1152]{2,1,0:T(8,128)(2,1)S(1)} %bitcast.36), channel_id=1, replica_groups=mesh['y'=8,'z'=8,'x'=4,'core'=2] {'core'}, dimensions={0} | all-to-all | bytes 2359296 | tf_op jit(solution)/shard_map/all_to_all | solution.py:446
  205.9 38.7 %all_to_all.53 = bf16[64,4,1152]{2,1,0:T(4,128)(2,1)S(1)} all-to-all(bf16[64,4,1152]{2,1,0:T(4,128)(2,1)S(1)} %reshape.161), channel_id=1, replica_groups=mesh['y'=8,'z'=8,'x'=4,'core'=2] {'y','z'}, dimensions={0} | all-to-all | bytes 1179648 | tf_op jit(solution)/shard_map/all_to_all | solution.py:446
  244.7 6.9 %all_to_all.54 = f32[4,4,1152]{2,1,0:T(4,128)S(1)} all-to-all(f32[4,4,1152]{2,1,0:T(4,128)S(1)} %broadcast_in_dim.71), channel_id=1, replica_groups=mesh['y'=8,'z'=8,'x'=4,'core'=2] {'x'}, dimensions={0} | all-to-all | bytes 147456 | tf_op jit(solution)/shard_map/all_to_all | solution.py:446
  251.7 24.6 %all_to_all.55 = bf16[64,4,1152]{2,1,0:T(4,128)(2,1)S(1)} all-to-all(bf16[64,4,1152]{2,1,0:T(4,128)(2,1)S(1)} %broadcast_in_dim.72), channel_id=1, replica_groups=mesh['y'=8,'z'=8,'x'=4,'core'=2] {'y','z'}, dimensions={0} | all-to-all | bytes 1179648 | tf_op jit(solution)/shard_map/all_to_all | solution.py:446
  276.5 9.3 %all_to_all.56 = bf16[2,256,1152]{2,1,0:T(8,128)(2,1)S(1)} all-to-all(bf16[2,256,1152]{2,1,0:T(8,128)(2,1)S(1)} %broadcast_in_dim.74), channel_id=1, replica_groups=mesh['y'=8,'z'=8,'x'=4,'core'=2] {'core'}, dimensions={0} | all-to-all | bytes 2359296 | tf_op jit(solution)/shard_map/all_to_all | solution.py:446
  287.0 1.6 slice_convert_fusion
  (58 shorter events, 4.7 us)
Async XLA Ops:
  7.2 1.7 copy-start
  7.2 146.5 %all-gather.3.cloned.1.call-start = ((), (), s32[]{:S(2)}) async-start(), calls=%async_computation.10 | async-start | bytes 3575808 | tf_op jit(solution)/shard_map/all_gather | solution.py:482
  8.9 1.2 copy-start.3
  69.0 8.2 %copy-start.7 = (bf16[2048,512]{1,0:T(8,128)(2,1)}, bf16[2048,512]{1,0:T(8,128)(2,1)S(1)}, u32[]{:S(2)}) copy-start(bf16[2048,512]{1,0:T(8,128)(2,1)S(1)} %pad_maximum_fusion) | copy-start | bytes 6291460
  77.2 9.4 %copy-start.9 = (f32[192,10]{0,1:T(8,128)S(1)}, f32[192,10]{0,1:T(8,128)}, u32[]{:S(2)}) copy-start(f32[192,10]{0,1:T(8,128)} %param.15) | copy-start | bytes 23044
  77.2 69.0 %all-to-all-start.2 = ((bf16[64,40,512]{2,1,0:T(8,128)(2,1)}), bf16[64,40,512]{2,1,0:T(8,128)(2,1)S(1)}, u32[]{:S(2)}, u32[]{:S(2)}) async-start(bf16[64,40,512]{2,1,0:T(8,128)(2,1)} %bitcast.43), calls=%async_computation.2 | async-start | bytes 5242880 | tf_op jit(solution)/shard_map/all_to_all | solution.py:446
  155.7 1.9 copy-start.1
  155.7 1.9 copy-start.5
  155.7 1.9 copy-start.6
  157.6 1.2 copy-start.2
  184.1 10.1 %copy-start.4 = (bf16[192,1024]{1,0:T(8,128)(2,1)S(1)}, bf16[192,1024]{1,0:T(8,128)(2,1)}, u32[]{:S(2)}) copy-start(bf16[192,1024]{1,0:T(8,128)(2,1)} %get-tuple-element.34.embedded_ref) | copy-start | bytes 1179652
  184.1 10.1 %copy-start.8 = (bf16[2112,512]{1,0:T(8,128)(2,1)S(1)}, bf16[2112,512]{1,0:T(8,128)(2,1)}, u32[]{:S(2)}) copy-start(bf16[2112,512]{1,0:T(8,128)(2,1)} %get-tuple-element.60.own_ref.near_ref.fetched_ref) | copy-start | bytes 6488068
Sparse Core Ops, SparseCore 0:
  68.7 32.6 all-gather.2

commit v6 on v5

--- a/solution.py
+++ b/solution.py
@@ -12,8 +12,8 @@
 SLOTS = 40
 ALL_SLOTS = 80
 PIECE = 16
-COPIED = 12
-TARGETS = (42, 34, 38, 36, 40, 38, 40, 40)
+COPIED = 13
+TARGETS = (44, 36, 38, 39, 40)
 DIGIT = 32
 PER = 5
 CHUNK = 256
@@ -486,7 +486,7 @@
         return jnp.roll(values.reshape(targets, K + 1).T, -1, axis=0).reshape(-1)
 
     target, slot = ordered(target), ordered(slot)
-    late = slot >= SLOTS
+    late = over & (slot >= SLOTS)
     fetched = jnp.take(got, jnp.where(late, 0, target * SLOTS + slot), axis=0, mode="clip")
 
     def second_exchange(fetched):

time: 298 us -> 295 us (0.990)
    all_to_all x1, waiting for transfers between devices: 58.4 us -> 42.9 us  [exchange(): return lax.all_to_all(values, axes, split_axis=0, concat_axis=0, tiled=True)]
    all_gather x1, waiting for transfers between devices: 0.01 us -> 13.5 us  [body(): w_full = lax.all_gather(w_part, GRP, axis=0, tiled=False)]
  transfers between devices with their start and end apart: 2 -> 2, of which waited for: 1 -> 2; matrix products, arithmetic and copies ran while one was open for 6% -> 4% of each run, Pallas kernels for 0% -> 0%
where the time goes in v6:
time: 295 us; the launch traced here: 294 us
  blocking collectives  160 us (54%)
  waiting for transfers between devices  56.5 us (19%)
  local copies, waits for them, and re-layouts  24.7 us (8%)
  Pallas kernels  20 us (7%)
  between operations  16.8 us (6%)
  starting transfers between devices  9.44 us (3%)
  other arithmetic  6.28 us (2%)
    all_to_all x8, blocking collectives, exchange(): return lax.all_to_all(values, axes, split_axis=0, concat_axis=0, tiled=True)  160 us
    all_to_all x1, waiting for transfers between devices, exchange(): return lax.all_to_all(values, axes, split_axis=0, concat_axis=0, tiled=True)  42.9 us
    all_gather x1, waiting for transfers between devices, body(): w_full = lax.all_gather(w_part, GRP, axis=0, tiled=False)  13.5 us
    all_to_all x1, starting transfers between devices, exchange(): return lax.all_to_all(values, axes, split_axis=0, concat_axis=0, tiled=True)  9.4 us
    pallas_call x1, Pallas kernels, forward(): pl.pallas_call(forward_kernel, grid=(K // PER,), in_specs=[pl.BlockSpec((...  8.28 us
    gather x1, local copies, waits for them, and re-layouts, body(): picked = jnp.take(table, asked[:, :SLOTS].reshape(-1), axis=0, mode='clip')  8.22 us
    gather x1, local copies, waits for them, and re-layouts, body(): jnp.take(got, jnp.where(late, 0, target * SLOTS + slot), axis=0, mode='cl...  7.44 us
    pallas_call x1, Pallas kernels, backward(): pl.pallas_call(backward_kernel, in_specs=[near, near, far, far, near, nea...  6.6 us
  transfers between devices with their start and end apart: 2, of which 2 were waited for; matrix products, arithmetic and copies ran while one was open for 4% of the time, Pallas kernels for 0%

profile of v6, /device:TPU:1, one launch (start us, length us, event | category | flops | bytes accessed | tf_op | source)
XLA Modules:
  0.0 293.9 jit_solution(8149558850201396376)
XLA Ops:
  7.2 0.7 add_reduce_fusion
  8.0 0.9 copy.59.scales_ref
  8.9 1.2 copy-done.3
  10.2 5.1 %plan.1 = (bf16[1024,640]{1,0:T(8,128)(2,1)S(1)}, bf16[1024,512]{1,0:T(8,128)(2,1)S(1)}, s32[17,128]{1,0:T(8,128)S(1)}, s32[17,128]{1,0:T(8,128)S(1)}) custom-call(s32[17,128]{1,0:T(8,128)S(1)} %pad_bitcast_fusion.row_ref, bf16[1024,512]{1,0:T(8,128)(2,1)S(1)} %copy-done.3, bf16[1024,4]{1,0:T(8,128)(2,1)S(1)} %copy.59.scales_ref, ...), custom_call_target="tpu_custom_call" | custom-call | tf_op jit(solution)/shard_map/plan/pallas_call | solution.py:176
  15.3 49.1 %all_to_all.49 = bf16[64,16,640]{2,1,0:T(8,128)(2,1)S(1)} all-to-all(bf16[64,16,640]{2,1,0:T(8,128)(2,1)S(1)} %bitcast.37), channel_id=1, replica_groups=mesh['y'=8,'z'=8,'x'=4,'core'=2] {'y','z'}, dimensions={0} | all-to-all | bytes 2621440 | tf_op jit(solution)/shard_map/all_to_all | solution.py:446
  65.5 1.4 concatenate.17
  67.5 8.2 %gather_fusion.2 = bf16[2560,512]{1,0:T(8,128)(2,1)} fusion(bf16[2048,512]{1,0:T(8,128)(2,1)S(1)} %pad_maximum_fusion, s32[3072]{0:T(1024)S(1)} %pad_clamp_fusion.3), kind=kCustom, calls=%fused_computation.2 | custom fusion | bytes 5253120 | tf_op jit(solution)/shard_map/jit(_take)/gather | solution.py:475
  75.7 9.4 %all-to-all-start.2 = ((bf16[64,40,512]{2,1,0:T(8,128)(2,1)}), bf16[64,40,512]{2,1,0:T(8,128)(2,1)S(1)}, u32[]{:S(2)}, u32[]{:S(2)}) async-start(bf16[64,40,512]{2,1,0:T(8,128)(2,1)} %bitcast.43), calls=%async_computation.2 | async-start | bytes 5242880 | tf_op jit(solution)/shard_map/all_to_all | solution.py:446
  86.2 13.5 %all-gather.3.cloned.1.call-done = bf16[12416,128]{1,0:T(8,128)(2,1)} async-done(((bf16[1552,128]{1,0:T(8,128)(2,1)}), bf16[12416,128]{1,0:T(8,128)(2,1)}) %all-gather.3.cloned.1.call-update) | async-done | bytes 3178512 | tf_op jit(solution)/shard_map/all_gather | solution.py:482
  99.7 1.3 slice_reduce_fusion.1
  101.8 42.9 %all-to-all-done.2 = bf16[64,40,512]{2,1,0:T(8,128)(2,1)S(1)} async-done(((bf16[64,40,512]{2,1,0:T(8,128)(2,1)}), bf16[64,40,512]{2,1,0:T(8,128)(2,1)S(1)}, u32[]{:S(2)}, u32[]{:S(2)}) %all-to-all-start.2) | async-done | bytes 2621472 | tf_op jit(solution)/shard_map/all_to_all | solution.py:446
  144.7 7.4 %gather_fusion.3 = bf16[2112,512]{1,0:T(8,128)(2,1)} fusion(bf16[2560,512]{1,0:T(8,128)(2,1)S(1)} %bitcast.42, s32[3072]{0:T(1024)S(1)} %pad_clamp_fusion.2), kind=kCustom, calls=%fused_computation.3 | custom fusion | bytes 4333824 | tf_op jit(solution)/shard_map/jit(_take)/gather | solution.py:490
  152.3 1.7 copy-done.1
  154.0 1.2 copy-done.2
  155.3 8.3 %forward.1 = (bf16[1920,1024]{1,0:T(8,128)(2,1)S(1)}, bf16[192,1024]{1,0:T(8,128)(2,1)}, f32[192,1024]{1,0:T(8,128)S(1)}, f32[192,1024]{1,0:T(8,128)S(1)}, bf16[128,1152]{1,0:T(8,128)(2,1)S(1)}) custom-call(bf16[2112,512]{1,0:T(8,128)(2,1)} %get-tuple-element.67.own_ref.near_ref.fetched_ref, ...), custom_call_target="tpu_custom_call" | custom-call | tf_op jit(solution)/shard_map/forward/pallas_call | solution.py:296
  163.6 16.3 %all_to_all.50 = bf16[4,128,1152]{2,1,0:T(8,128)(2,1)S(1)} all-to-all(bf16[4,128,1152]{2,1,0:T(8,128)(2,1)S(1)} %broadcast_in_dim.69), channel_id=1, replica_groups=mesh['y'=8,'z'=8,'x'=4,'core'=2] {'x'}, dimensions={0} | all-to-all | bytes 2359296 | tf_op jit(solution)/shard_map/all_to_all | solution.py:446
  180.3 10.3 %all_to_all.51 = bf16[2,4,128,1152]{3,2,1,0:T(8,128)(2,1)S(1)} all-to-all(bf16[2,4,128,1152]{3,2,1,0:T(8,128)(2,1)S(1)} %broadcast_in_dim.70), channel_id=1, replica_groups=mesh['y'=8,'z'=8,'x'=4,'core'=2] {'core'}, dimensions={0} | all-to-all | bytes 4718592 | tf_op jit(solution)/shard_map/all_to_all | solution.py:446
  190.6 6.6 %backward.1 = bf16[512,1152]{1,0:T(8,128)(2,1)S(1)} custom-call(bf16[2112,512]{1,0:T(8,128)(2,1)S(1)} %copy-done.8, f32[192,10]{1,0:T(8,128)S(1)} %copy.64.importance_ref, bf16[8,1552,128]{2,1,0:T(8,128)(2,1)S(1)} %bitcast.34, bf16[1920,1024]{1,0:T(8,128)(2,1)S(1)} %get-tuple-element.48.slope_far_ref, bf16[192,1024]{1,0:T(8,128)(2,1)S(1)} %copy-done.4, ...), custom_call_target="tpu_custom_call" | custom-call | tf_op jit(solution)/shard_map/backward/pallas_call | solution.py:428
  197.2 4.7 %all_to_all.52 = bf16[2,256,1152]{2,1,0:T(8,128)(2,1)S(1)} all-to-all(bf16[2,256,1152]{2,1,0:T(8,128)(2,1)S(1)} %bitcast.36), channel_id=1, replica_groups=mesh['y'=8,'z'=8,'x'=4,'core'=2] {'core'}, dimensions={0} | all-to-all | bytes 2359296 | tf_op jit(solution)/shard_map/all_to_all | solution.py:446
  202.3 39.0 %all_to_all.53 = bf16[64,4,1152]{2,1,0:T(4,128)(2,1)S(1)} all-to-all(bf16[64,4,1152]{2,1,0:T(4,128)(2,1)S(1)} %reshape.171), channel_id=1, replica_groups=mesh['y'=8,'z'=8,'x'=4,'core'=2] {'y','z'}, dimensions={0} | all-to-all | bytes 1179648 | tf_op jit(solution)/shard_map/all_to_all | solution.py:446
  241.4 6.9 %all_to_all.54 = f32[4,4,1152]{2,1,0:T(4,128)S(1)} all-to-all(f32[4,4,1152]{2,1,0:T(4,128)S(1)} %broadcast_in_dim.71), channel_id=1, replica_groups=mesh['y'=8,'z'=8,'x'=4,'core'=2] {'x'}, dimensions={0} | all-to-all | bytes 147456 | tf_op jit(solution)/shard_map/all_to_all | solution.py:446
  248.4 24.6 %all_to_all.55 = bf16[64,4,1152]{2,1,0:T(4,128)(2,1)S(1)} all-to-all(bf16[64,4,1152]{2,1,0:T(4,128)(2,1)S(1)} %broadcast_in_dim.72), channel_id=1, replica_groups=mesh['y'=8,'z'=8,'x'=4,'core'=2] {'y','z'}, dimensions={0} | all-to-all | bytes 1179648 | tf_op jit(solution)/shard_map/all_to_all | solution.py:446
  273.2 9.3 %all_to_all.56 = bf16[2,256,1152]{2,1,0:T(8,128)(2,1)S(1)} all-to-all(bf16[2,256,1152]{2,1,0:T(8,128)(2,1)S(1)} %broadcast_in_dim.74), channel_id=1, replica_groups=mesh['y'=8,'z'=8,'x'=4,'core'=2] {'core'}, dimensions={0} | all-to-all | bytes 2359296 | tf_op jit(solution)/shard_map/all_to_all | solution.py:446
  283.7 1.6 slice_convert_fusion
  (58 shorter events, 5.4 us)
Async XLA Ops:
  7.2 1.7 copy-start
  7.2 92.5 %all-gather.3.cloned.1.call-start = ((), (), s32[]{:S(2)}) async-start(), calls=%async_computation.10 | async-start | bytes 3575808 | tf_op jit(solution)/shard_map/all_gather | solution.py:482
  8.9 1.2 copy-start.3
  67.4 8.2 %copy-start.7 = (bf16[2048,512]{1,0:T(8,128)(2,1)}, bf16[2048,512]{1,0:T(8,128)(2,1)S(1)}, u32[]{:S(2)}) copy-start(bf16[2048,512]{1,0:T(8,128)(2,1)S(1)} %pad_maximum_fusion) | copy-start | bytes 6291460
  75.7 9.4 %copy-start.9 = (f32[192,10]{0,1:T(8,128)S(1)}, f32[192,10]{0,1:T(8,128)}, u32[]{:S(2)}) copy-start(f32[192,10]{0,1:T(8,128)} %param.15) | copy-start | bytes 23044
  75.7 69.0 %all-to-all-start.2 = ((bf16[64,40,512]{2,1,0:T(8,128)(2,1)}), bf16[64,40,512]{2,1,0:T(8,128)(2,1)S(1)}, u32[]{:S(2)}, u32[]{:S(2)}) async-start(bf16[64,40,512]{2,1,0:T(8,128)(2,1)} %bitcast.43), calls=%async_computation.2 | async-start | bytes 5242880 | tf_op jit(solution)/shard_map/all_to_all | solution.py:446
  152.1 1.9 copy-start.1
  152.1 1.9 copy-start.5
  152.1 1.9 copy-start.6
  154.0 1.2 copy-start.2
  180.3 10.4 %copy-start.4 = (bf16[192,1024]{1,0:T(8,128)(2,1)S(1)}, bf16[192,1024]{1,0:T(8,128)(2,1)}, u32[]{:S(2)}) copy-start(bf16[192,1024]{1,0:T(8,128)(2,1)} %get-tuple-element.39.embedded_ref) | copy-start | bytes 1179652
  180.3 10.3 %copy-start.8 = (bf16[2112,512]{1,0:T(8,128)(2,1)S(1)}, bf16[2112,512]{1,0:T(8,128)(2,1)}, u32[]{:S(2)}) copy-start(bf16[2112,512]{1,0:T(8,128)(2,1)} %get-tuple-element.67.own_ref.near_ref.fetched_ref) | copy-start | bytes 6488068
Sparse Core Ops, SparseCore 0:
  67.0 32.5 all-gather.2
